TPU v7x, 128 devices: a whole 4x4x4 slice. The times are simulated.
128 devices in a mesh: row: 8 (over y, core), col: 16 (over x, z).
Axes of the slice: x: 4, y: 4, z: 4, core: 2. Of those that a mesh axis runs over, the one named last changes fastest.
Arguments:
- amplitudes: bfloat16 [12288, 8192], P(('row', 'col')), may hold values from -6 to 6
- integrals: bfloat16 [8192, 8192], P('row', 'col'), may hold values from -0.09375 to 0.09375
- amplitude_mask: int32 [12288, 64], P(('row', 'col')), may hold values from 0 to 1, as said below
- integral_mask: int32 [64, 64], P('row', 'col'), may hold values from 0 to 1
Outputs:
- ladder: bfloat16 [12288, 8192], P('row', 'col')
Inputs may be any that keep to these rules, and one draw needn't show every extreme that they name: `amplitude_mask`: in every row the kept tiles form one cyclic band of consecutive tiles, 1 to 40 of them; some row keeps exactly 40.
All inputs are finite; a program needn't handle non-finite values.
Results may differ from a plain program's by a relative error of at most 0.001.
Values may be sent and summed in bfloat16 or wider, within the bound.
No kernel may reach another device: no remote copies, remote signals or barrier semaphores. Data moves between devices by JAX's collectives and lax.ppermute only.
A program may use at most 128 MiB of HBM per device.

v0:
```python
import jax
import jax.numpy as jnp
from jax import lax
from jax.sharding import PartitionSpec as P

TILE = 128


def on_device(amplitudes, integrals, amplitude_mask, integral_mask):
    amp_keep = jnp.repeat(amplitude_mask, TILE, axis=1).astype(jnp.bfloat16)
    kept_amps = amplitudes * amp_keep
    int_keep = jnp.repeat(jnp.repeat(integral_mask, TILE, axis=0), TILE, axis=1).astype(
        jnp.bfloat16
    )
    kept_ints = integrals * int_keep
    row_amps = lax.all_gather(kept_amps, "col", axis=0, tiled=True)
    result = jnp.dot(
        row_amps,
        lax.all_gather(kept_ints, "row", axis=0, tiled=True),
        preferred_element_type=jnp.float32,
    )
    return result.astype(jnp.bfloat16)


def solution(mesh):
    in_specs = (P(("row", "col"), None), P("row", "col"), P(("row", "col"), None), P("row", "col"))
    out_specs = P("row", "col")
    return jax.shard_map(
        on_device, mesh=mesh, in_specs=in_specs, out_specs=out_specs, check_vma=False
    )
```

profile of v0, /device:TPU:34, one launch (start us, length us, event | category | flops | bytes accessed | tf_op | source)
XLA Modules:
  0.0 246.9 jit_solution(4406139277438614595)
XLA Ops:
  6.5 0.0 copy-start.1
  6.5 0.0 all-gather.5.cloned.1.call-start
  6.5 0.7 convert_element_type.23
  7.2 0.1 copy.6
  7.4 2.9 %broadcast_in_dim.11 = bf16[1024,4,128]{2,1,0:T(4,128)(2,1)S(1)} broadcast(bf16[1024,4]{1,0:T(8,128)(2,1)S(1)} %bitcast.11), dimensions={0,1} | broadcast | bytes 1056768 | tf_op jit(solution)/shard_map/broadcast_in_dim | solution.py:12
  10.3 0.0 copy-start
  10.3 2.5 bitcast_multiply_fusion.1
  12.8 0.0 all-gather.5.cloned.1.call-update
  12.8 0.0 all-gather.3.cloned.1.call-start
  12.9 0.0 copy-done.1
  12.9 0.1 copy.5
  13.0 1.0 broadcast_in_dim.9
  14.0 0.0 copy-done
  14.0 2.1 bitcast_multiply_fusion
  16.1 0.0 all-gather.3.cloned.1.call-update
  16.1 48.6 %all-gather.5.cloned.1.call-done = bf16[8192,512]{1,0:T(8,128)(2,1)} async-done(((bf16[1024,512]{1,0:T(8,128)(2,1)}), bf16[8192,512]{1,0:T(8,128)(2,1)}) %all-gather.5.cloned.1.call-update) | async-done | bytes 8388624 | tf_op jit(solution)/shard_map/all_gather | solution.py:19
  64.7 155.4 %all-gather.3.cloned.1.call-done = bf16[1536,8192]{1,0:T(8,128)(2,1)} async-done(((bf16[96,8192]{1,0:T(8,128)(2,1)}), bf16[1536,8192]{1,0:T(8,128)(2,1)}) %all-gather.3.cloned.1.call-update) | async-done | bytes 25165840 | tf_op jit(solution)/shard_map/all_gather | solution.py:16
  220.1 20.0 %convolution_convert_fusion = bf16[1536,512]{1,0:T(8,128)(2,1)} fusion(bf16[1536,8192]{1,0:T(8,128)(2,1)} %all-gather.3.cloned.1.call-done, bf16[8192,512]{1,0:T(8,128)(2,1)} %all-gather.5.cloned.1.call-done), kind=kOutput, calls=%fused_computation | convolution fusion | flops 12885688320 | bytes 35127296 | tf_op jit(solution)/shard_map/dot_general | solution.py:17
  (2 shorter events, 0.0 us)
Async XLA Ops:
  6.5 6.3 %copy-start.1 = (s32[96,64]{0,1:T(8,128)S(1)}, s32[96,64]{0,1:T(8,128)}, u32[]{:S(2)}) copy-start(s32[96,64]{0,1:T(8,128)} %param.6) | copy-start | bytes 73732
  6.5 58.2 %all-gather.5.cloned.1.call-start = ((), (), s32[]{:S(2)}) async-start(), calls=%async_computation.1 | async-start | bytes 9437184 | tf_op jit(solution)/shard_map/all_gather | solution.py:19
  10.3 3.7 %copy-start = (bf16[96,8192]{1,0:T(8,128)(2,1)S(1)}, bf16[96,8192]{1,0:T(8,128)(2,1)}, u32[]{:S(2)}) copy-start(bf16[96,8192]{1,0:T(8,128)(2,1)} %param.4) | copy-start | bytes 4718596
  12.8 207.2 %all-gather.3.cloned.1.call-start = ((), (), s32[]{:S(2)}) async-start(), calls=%async_computation | async-start | bytes 26738688 | tf_op jit(solution)/shard_map/all_gather | solution.py:16
Sparse Core Ops, SparseCore 0:
  12.9 51.7 all-gather.4
  66.9 153.1 all-gather.2
where the time goes:
time: 250 us; the launch traced here: 247 us
  waiting for transfers between devices  204 us (82%)
  matrix products  20 us (8%)
  between operations  13.5 us (5%)
  other arithmetic  5.28 us (2%)
  local copies, waits for them, and re-layouts  4.17 us (2%)
    all_gather x1, waiting for transfers between devices, on_device(): row_amps = lax.all_gather(kept_amps, 'col', axis=0, tiled=True)  155 us
    all_gather x1, waiting for transfers between devices, on_device(): lax.all_gather(kept_ints, 'row', axis=0, tiled=True)  48.6 us
    dot_general x1, matrix products, on_device(): jnp.dot(row_amps, lax.all_gather(kept_ints, 'row', axis=0, tiled=True), p...  20 us
  transfers between devices with their start and end apart: 2, of which 2 were waited for; matrix products, arithmetic and copies ran while one was open for 1% of the time, Pallas kernels for 0%

commit v1 on v0

v1 whole, which is shorter than its diff:
```python
import functools

import jax
import jax.numpy as jnp
from jax import lax
from jax.experimental import pallas as pl
from jax.experimental.pallas import tpu as pltpu
from jax.sharding import PartitionSpec as P

TILE = 128
KT = 64
SLOTS = 40
FOLD = KT - SLOTS
WIDE = (SLOTS + 1) * TILE
BF = jnp.bfloat16


def pack_kernel(mask_ref, amps_ref, *outs):
    rows = amps_ref.shape[0]
    mask = mask_ref[...]
    tile = lax.broadcasted_iota(jnp.int32, mask.shape, 1)
    count = jnp.sum(mask, axis=1, keepdims=True)
    low = jnp.min(jnp.where(mask > 0, tile, KT), axis=1, keepdims=True)
    high = jnp.max(jnp.where(mask > 0, tile, -1), axis=1, keepdims=True)
    end = jnp.min(jnp.where(mask > 0, KT, tile), axis=1, keepdims=True)
    wraps = high - low + 1 > count
    alpha = jnp.where(wraps, 0, jnp.minimum(low, FOLD))
    beta = jnp.where(wraps, end, SLOTS)
    first = jnp.where(wraps, end + KT - count, low)
    last = jnp.where(wraps, KT, high + 1)
    wide = lambda v: jnp.broadcast_to(v.astype(jnp.float32), (rows, TILE)).astype(BF)
    code = wide(jnp.where(wraps, -end, alpha))
    alpha, beta, first, last = wide(alpha), wide(beta), wide(first), wide(last)
    zero = jnp.zeros((rows, TILE), BF)

    def tile_of(t):
        return amps_ref[:, t * TILE : (t + 1) * TILE]

    def put(j, value):
        row = 0
        for out in outs:
            n = out.shape[0]
            out[:, j * TILE : (j + 1) * TILE] = value[row : row + n]
            row += n

    for j in range(SLOTS):
        value = jnp.where((first <= j) & (j < last), tile_of(j), zero)
        value = jnp.where((beta < SLOTS) & (j < beta), tile_of(j), value)
        far = jnp.where((first <= j + FOLD) & (j + FOLD < last), tile_of(j + FOLD), zero)
        value = jnp.where(beta <= j, far, value)
        if j < FOLD:
            up = jnp.where((first <= j + SLOTS) & (j + SLOTS < last), tile_of(j + SLOTS), zero)
            value = jnp.where(j < alpha, up, value)
        put(j, value)
    put(SLOTS, code)


def ints_kernel(mask_ref, ints_ref, kept_ref):
    for i in range(ints_ref.shape[0] // TILE):
        for j in range(ints_ref.shape[1] // TILE):
            at = (slice(i * TILE, (i + 1) * TILE), slice(j * TILE, (j + 1) * TILE))
            keep = jnp.full((TILE, TILE), mask_ref[j, i].astype(jnp.float32), jnp.float32).astype(BF)
            kept_ref[at] = ints_ref[at] * keep


def mm_kernel(n_in, parts, *refs):
    offs = refs[0]
    amps = refs[1 : 1 + n_in]
    ints = refs[1 + n_in]
    out, wide, done, sem = refs[-4:]
    starts, at = [], 0
    for part in parts:
        starts.append(at)
        at += part[2]

    def place(part):
        return pl.multiple_of(offs[part[3]] + part[4], 16)

    for part, p in zip(parts, starts):
        a, row0, rows = part[:3]
        code = amps[a][row0 : row0 + rows, SLOTS * TILE :]
        zero = jnp.zeros((rows, TILE), BF)
        alpha = jnp.where(code < 0, zero, code)
        beta = jnp.where(code < 0, zero - code, zero + SLOTS)

        def slot(j):
            return amps[a][row0 : row0 + rows, j * TILE : (j + 1) * TILE]

        for t in range(KT):
            if t < FOLD:
                v = jnp.where((alpha <= t) & (t < beta), slot(t), zero)
            elif t < SLOTS:
                v = jnp.where(t < beta, slot(t), zero)
                v = jnp.where(beta <= t - FOLD, slot(t - FOLD), v)
            else:
                v = jnp.where(t - SLOTS < alpha, slot(t - SLOTS), zero)
                v = jnp.where(beta <= t - FOLD, slot(t - FOLD), v)
            wide[p : p + rows, t * TILE : (t + 1) * TILE] = v

    done[...] = jnp.dot(wide[...], ints[...], preferred_element_type=jnp.float32).astype(BF)
    copies = [
        pltpu.make_async_copy(done.at[pl.ds(p, part[2])], out.at[pl.ds(place(part), part[2])], sem)
        for part, p in zip(parts, starts)
    ]
    for c in copies:
        c.start()
    for c in copies:
        c.wait()


def multiply(amps, parts, offs, ints, out, out_rows):
    rows = sum(p[2] for p in parts)
    cols = ints.shape[1]
    whole = pl.BlockSpec(memory_space=pltpu.VMEM)
    in_specs = [pl.BlockSpec(memory_space=pltpu.SMEM)] + [whole] * (len(amps) + 1)
    args = [offs] + list(amps) + [ints]
    alias = {}
    if out is not None:
        in_specs.append(pl.BlockSpec(memory_space=pl.ANY))
        alias = {len(args): 0}
        args.append(out)
    return pl.pallas_call(
        functools.partial(mm_kernel, len(amps), tuple(parts)),
        out_shape=jax.ShapeDtypeStruct((out_rows, cols), BF),
        in_specs=in_specs,
        out_specs=pl.BlockSpec(memory_space=pl.ANY),
        scratch_shapes=[
            pltpu.VMEM((rows, KT * TILE), BF),
            pltpu.VMEM((rows, cols), BF),
            pltpu.SemaphoreType.DMA,
        ],
        input_output_aliases=alias,
        compiler_params=pltpu.CompilerParams(vmem_limit_bytes=14 * 2**20),
        cost_estimate=pl.CostEstimate(
            flops=2 * rows * KT * TILE * cols,
            bytes_accessed=2 * (rows * WIDE + KT * TILE * cols + rows * cols),
            transcendentals=0,
        ),
    )(*args)


def pack(mask, amps):
    rows = amps.shape[0]
    sizes = [rows]
    return pl.pallas_call(
        pack_kernel,
        out_shape=[jax.ShapeDtypeStruct((n, WIDE), BF) for n in sizes],
    )(mask, amps)


def mask_ints(mask, ints):
    return pl.pallas_call(
        ints_kernel,
        out_shape=jax.ShapeDtypeStruct(ints.shape, ints.dtype),
        in_specs=[pl.BlockSpec(memory_space=pltpu.SMEM), pl.BlockSpec(memory_space=pltpu.VMEM)],
        out_specs=pl.BlockSpec(memory_space=pltpu.VMEM),
    )(mask.T, ints)


def moves(nx, nz, n_row):
    def shift(dx, dz):
        pairs = []
        for r in range(n_row):
            s = 1 - 2 * (r % 2)
            for x in range(nx):
                for z in range(nz):
                    to = (x + s * dx) % nx * nz + (z + s * dz) % nz
                    pairs.append((r * nx * nz + x * nz + z, r * nx * nz + to))
        return pairs

    return shift(1, 0), shift(-1, 0), shift(0, 1), shift(0, -1)


def on_device(amplitudes, integrals, amplitude_mask, integral_mask):
    dev_rows = amplitudes.shape[0]
    own = pack(amplitude_mask, amplitudes)[0]
    kept_ints = mask_ints(integral_mask, integrals)
    all_ints = lax.all_gather(kept_ints, "row", axis=0, tiled=True)
    half = dev_rows // 2
    xf, xb, zf, zb = moves(4, 4, 8)
    go = lambda v, perm: lax.ppermute(v, ("row", "col"), perm)
    x_m, z_m = go(own, xf), go(own, zf)
    x_p, z_p = go(own, xb), go(own, zb)
    x2, mm = go(x_m, xf), go(x_m, zf)
    pm, pp = go(z_m, xb), go(x_p, zb)
    mp, z2 = go(z_p, xf), go(z_m, zf)
    x2p, pz2 = go(pp, xb), go(pp, zb)
    mz2, x2m = go(z2, xf), go(x2, zf)
    far_a, far_b = go(pz2[:half], xb), go(x2p[half:], zb)

    me = lax.axis_index("col")
    sign = 1 - 2 * (lax.axis_index("row") % 2)
    x, z = me // 4, me % 4
    at = lambda dx, dz: ((x + sign * dx + 4) % 4 * 4 + (z + sign * dz + 4) % 4) * dev_rows
    total = 16 * dev_rows

    def call(blocks, out):
        arrays = [b[0] for b in blocks]
        offs = jnp.stack([at(*b[1]) for b in blocks]).astype(jnp.int32)
        parts = [(i, 0, b[0].shape[0], i, b[2]) for i, b in enumerate(blocks)]
        return multiply(arrays, parts, offs, all_ints, out, total)

    out = call([(own, (0, 0), 0), (x_m, (-1, 0), 0), (z_m, (0, -1), 0), (x_p, (1, 0), 0), (z_p, (0, 1), 0)], None)
    out = call([(x2, (2, 0), 0), (mm, (-1, -1), 0), (pm, (1, -1), 0), (pp, (1, 1), 0)], out)
    out = call([(mp, (-1, 1), 0), (z2, (0, 2), 0), (x2p, (2, 1), 0), (pz2, (1, 2), 0)], out)
    out = call([(mz2, (-1, 2), 0), (x2m, (2, -1), 0), (far_a, (2, 2), 0), (far_b, (2, 2), half)], out)
    return out


def solution(mesh):
    in_specs = (P(("row", "col"), None), P("row", "col"), P(("row", "col"), None), P("row", "col"))
    out_specs = P("row", "col")
    return jax.shard_map(
        on_device, mesh=mesh, in_specs=in_specs, out_specs=out_specs, check_vma=False
    )
```

time: 250 us -> 143 us (0.57)
  the two profiles are of different devices: /device:TPU:34 before, /device:TPU:0 now
where the time goes in v1:
time: 143 us; the launch traced here: 142 us
  waiting for transfers between devices  61.9 us (43%)
  Pallas kernels  31.3 us (22%)
  starting transfers between devices  28.2 us (20%)
  between operations  13.5 us (9%)
  local copies, waits for them, and re-layouts  7.28 us (5%)
    ppermute x16, waiting for transfers between devices, on_device(): go = lambda v, perm: lax.ppermute(v, ('row', 'col'), perm)  61.8 us
    ppermute x16, starting transfers between devices, on_device(): go = lambda v, perm: lax.ppermute(v, ('row', 'col'), perm)  28.2 us
    pallas_call x4, Pallas kernels, multiply(): pl.pallas_call(functools.partial(mm_kernel, len(amps), tuple(parts)), out...  25.5 us
    unnamed x15, local copies, waits for them, and re-layouts  6.32 us
    pallas_call x1, Pallas kernels, pack(): pl.pallas_call(pack_kernel, out_shape=[jax.ShapeDtypeStruct((n, WIDE), BF...  3.36 us
  transfers between devices with their start and end apart: 17, of which 5 were waited for; matrix products, arithmetic and copies ran while one was open for 1% of the time, Pallas kernels for 17%

profile of v1, /device:TPU:0, one launch (start us, length us, event | category | flops | bytes accessed | tf_op | source)
XLA Modules:
  0.0 142.5 jit_solution(16756223701981153303)
XLA Ops:
  6.5 2.4 %shard_map.47 = bf16[1024,512]{1,0:T(8,128)(2,1)} custom-call(s32[4,8]{1,0:T(4,128)} %bitcast.17, bf16[1024,512]{1,0:T(8,128)(2,1)} %ints_ref.1), custom_call_target="tpu_custom_call" | custom-call | tf_op jit(solution)/shard_map/pallas_call | solution.py:152
  8.9 0.0 all-gather.2.cloned.1.call-update
  9.0 0.7 copy.8.mask_ref
  9.7 3.4 %shard_map.46.refs_1_ = bf16[96,5248]{1,0:T(8,128)(2,1)} custom-call(s32[96,64]{1,0:T(8,128)} %copy.8.mask_ref, bf16[96,8192]{1,0:T(8,128)(2,1)} %amps_ref.1), custom_call_target="tpu_custom_call" | custom-call | tf_op jit(solution)/shard_map/pallas_call | solution.py:145
  13.0 2.8 %collective-permute-start.6 = (bf16[96,5248]{1,0:T(8,128)(2,1)}, bf16[96,5248]{1,0:T(8,128)(2,1)S(1)}, u32[]{:S(2)}, u32[]{:S(2)}) collective-permute-start(bf16[96,5248]{1,0:T(8,128)(2,1)} %shard_map.46.refs_1_), channel_id=1, source_target_pairs={{0,12},{1,13},{2,14},{3,15},{4,0},{5,1},{6,2},{7,3},{8,4},{9,5},{1... | collective-permute-start | bytes 3022856 | tf_op jit(solution)/shard_map/ppermute | solution.py:181
  15.9 0.0 collective-permute-start.3
  15.9 1.9 %collective-permute-start = (bf16[96,5248]{1,0:T(8,128)(2,1)}, bf16[96,5248]{1,0:T(8,128)(2,1)}, u32[]{:S(2)}, u32[]{:S(2)}) collective-permute-start(bf16[96,5248]{1,0:T(8,128)(2,1)} %shard_map.46.refs_1_), channel_id=1, source_target_pairs={{0,1},{1,2},{2,3},{3,0},{4,5},{5,6},{6,7},{7,4},{8,9},{9,10},{10,1... | collective-permute-start | bytes 3022856 | tf_op jit(solution)/shard_map/ppermute | solution.py:181
  17.8 20.4 %collective-permute-done.6.refs_4_ = bf16[96,5248]{1,0:T(8,128)(2,1)S(1)} collective-permute-done((bf16[96,5248]{1,0:T(8,128)(2,1)}, bf16[96,5248]{1,0:T(8,128)(2,1)S(1)}, u32[]{:S(2)}, u32[]{:S(2)}) %collective-permute-start.6) | collective-permute-done | bytes 1007648 | tf_op jit(solution)/shard_map/ppermute | solution.py:181
  38.2 4.2 %collective-permute-start.7 = (bf16[96,5248]{1,0:T(8,128)(2,1)S(1)}, bf16[96,5248]{1,0:T(8,128)(2,1)}, u32[]{:S(2)}, u32[]{:S(2)}) collective-permute-start(bf16[96,5248]{1,0:T(8,128)(2,1)S(1)} %collective-permute-done.6.refs_4_), channel_id=1, source_target_pairs={{0,3},{1,0},{2,1},{3,2},{4,7},{5,4},{6,5},{7,6},{8,11},{9,8},{10,9... | collective-permute-start | bytes 3022856 | tf_op jit(solution)/shard_map/ppermute | solution.py:181
  42.5 1.0 copy-done.3
  43.5 0.4 collective-permute-start.12
  43.9 0.0 collective-permute-done.3.refs_2_
  43.9 1.5 %collective-permute-start.4 = (bf16[96,5248]{1,0:T(8,128)(2,1)}, bf16[96,5248]{1,0:T(8,128)(2,1)}, u32[]{:S(2)}, u32[]{:S(2)}) collective-permute-start(bf16[96,5248]{1,0:T(8,128)(2,1)} %collective-permute-done.3.refs_2_), channel_id=1, source_target_pairs={{0,4},{1,5},{2,6},{3,7},{4,8},{5,9},{6,10},{7,11},{8,12},{9,13},{1... | collective-permute-start | bytes 3022856 | tf_op jit(solution)/shard_map/ppermute | solution.py:181
  45.4 0.0 collective-permute-done.refs_3_
  45.4 1.6 %collective-permute-start.1 = (bf16[96,5248]{1,0:T(8,128)(2,1)}, bf16[96,5248]{1,0:T(8,128)(2,1)}, u32[]{:S(2)}, u32[]{:S(2)}) collective-permute-start(bf16[96,5248]{1,0:T(8,128)(2,1)} %collective-permute-done.refs_3_), channel_id=1, source_target_pairs={{0,1},{1,2},{2,3},{3,0},{4,5},{5,6},{6,7},{7,4},{8,9},{9,10},{10,1... | collective-permute-start | bytes 3022856 | tf_op jit(solution)/shard_map/ppermute | solution.py:181
  47.0 16.7 %collective-permute-done.7.refs_4_ = bf16[96,5248]{1,0:T(8,128)(2,1)} collective-permute-done((bf16[96,5248]{1,0:T(8,128)(2,1)S(1)}, bf16[96,5248]{1,0:T(8,128)(2,1)}, u32[]{:S(2)}, u32[]{:S(2)}) %collective-permute-start.7) | collective-permute-done | bytes 1007648 | tf_op jit(solution)/shard_map/ppermute | solution.py:181
  63.7 3.8 %collective-permute-start.10 = (bf16[96,5248]{1,0:T(8,128)(2,1)}, bf16[96,5248]{1,0:T(8,128)(2,1)S(1)}, u32[]{:S(2)}, u32[]{:S(2)}) collective-permute-start(bf16[96,5248]{1,0:T(8,128)(2,1)} %collective-permute-done.7.refs_4_), channel_id=1, source_target_pairs={{0,12},{1,13},{2,14},{3,15},{4,0},{5,1},{6,2},{7,3},{8,4},{9,5},{1... | collective-permute-start | bytes 3022856 | tf_op jit(solution)/shard_map/ppermute | solution.py:181
  67.5 3.8 %collective-permute-start.8 = (bf16[96,5248]{1,0:T(8,128)(2,1)}, bf16[96,5248]{1,0:T(8,128)(2,1)S(1)}, u32[]{:S(2)}, u32[]{:S(2)}) collective-permute-start(bf16[96,5248]{1,0:T(8,128)(2,1)} %collective-permute-done.7.refs_4_), channel_id=1, source_target_pairs={{0,3},{1,0},{2,1},{3,2},{4,7},{5,4},{6,5},{7,6},{8,11},{9,8},{10,9... | collective-permute-start | bytes 3022856 | tf_op jit(solution)/shard_map/ppermute | solution.py:181
  71.3 6.2 %collective-permute-done.12.refs_5_ = bf16[96,5248]{1,0:T(8,128)(2,1)} collective-permute-done((bf16[96,5248]{1,0:T(8,128)(2,1)}, bf16[96,5248]{1,0:T(8,128)(2,1)}, u32[]{:S(2)}, u32[]{:S(2)}) %collective-permute-start.12) | collective-permute-done | bytes 1007648 | tf_op jit(solution)/shard_map/ppermute | solution.py:181
  77.5 0.2 collective-permute-start.14
  77.7 0.0 collective-permute-done.4.refs_1_
  77.7 2.7 %collective-permute-start.15 = (bf16[96,5248]{1,0:T(8,128)(2,1)}, bf16[96,5248]{1,0:T(8,128)(2,1)}, u32[]{:S(2)}, u32[]{:S(2)}) collective-permute-start(bf16[96,5248]{1,0:T(8,128)(2,1)} %collective-permute-done.refs_3_), channel_id=1, source_target_pairs={{0,12},{1,13},{2,14},{3,15},{4,0},{5,1},{6,2},{7,3},{8,4},{9,5},{1... | collective-permute-start | bytes 3022856 | tf_op jit(solution)/shard_map/ppermute | solution.py:181
  80.4 0.0 collective-permute-done.1.refs_2_
  80.4 0.0 collective-permute-start.13
  80.4 0.1 pad_add_fusion.refs_0_
  80.5 0.1 pad_add_fusion.2.refs_0_
  80.6 1.0 collective-permute-done.10.refs_3_
  81.6 0.0 collective-permute-start.2
  81.6 17.5 %collective-permute-done.8.refs_4_ = bf16[96,5248]{1,0:T(8,128)(2,1)S(1)} collective-permute-done((bf16[96,5248]{1,0:T(8,128)(2,1)}, bf16[96,5248]{1,0:T(8,128)(2,1)S(1)}, u32[]{:S(2)}, u32[]{:S(2)}) %collective-permute-start.8) | collective-permute-done | bytes 1007648 | tf_op jit(solution)/shard_map/ppermute | solution.py:181
  99.1 0.1 collective-permute-start.5
  99.2 0.1 pad_add_fusion.1.refs_0_
  99.2 0.1 stack.80.refs_0_
  99.3 0.8 slice.9
  100.2 0.0 all-gather.2.cloned.1.call-done.refs_6_.refs_5_
  100.3 3.4 %copy-done = bf16[8192,512]{1,0:T(8,128)(2,1)S(1)} copy-done((bf16[8192,512]{1,0:T(8,128)(2,1)S(1)}, bf16[8192,512]{1,0:T(8,128)(2,1)}, u32[]{:S(2)}) %copy-start) | copy-done | bytes 8388632
  103.6 1.2 copy-done.4
  104.8 7.4 %shard_map.48.refs_6_ = bf16[1536,512]{1,0:T(8,128)(2,1)} custom-call(s32[5]{0:T(128)S(1)} %stack.80.refs_0_, bf16[96,5248]{1,0:T(8,128)(2,1)S(1)} %copy-done.2, bf16[96,5248]{1,0:T(8,128)(2,1)} %collective-permute-done.3.refs_2_, bf16[96,5248]{1,0:T(8,128)(2,1)} %collective-permute-done.refs_3_, bf16[96,5248]{1,0:T(8,128)(2,1)S(1)} %copy-done.4, ...), custom_call_target="tpu_custom_call" | custom-call | flops 4026531840 | bytes 13918208 | tf_op jit(solution)/shard_map/pallas_call | solution.py:122
  112.3 0.0 collective-permute-done.14.refs_2_
  112.3 3.8 %collective-permute-start.11 = (bf16[48,5248]{1,0:T(8,128)(2,1)S(1)}, bf16[48,5248]{1,0:T(8,128)(2,1)S(1)}, u32[]{:S(2)}, u32[]{:S(2)}) collective-permute-start(bf16[48,5248]{1,0:T(8,128)(2,1)S(1)} %copy-done.5), channel_id=1, source_target_pairs={{0,3},{1,0},{2,1},{3,2},{4,7},{5,4},{6,5},{7,6},{8,11},{9,8},{10,9... | collective-permute-start | bytes 1511432 | tf_op jit(solution)/shard_map/ppermute | solution.py:181
  116.0 0.0 collective-permute-done.15.refs_3_
  116.0 1.4 collective-permute-start.9
  117.4 6.7 %shard_map.49.refs_6_ = bf16[1536,512]{1,0:T(8,128)(2,1)} custom-call(s32[4]{0:T(128)S(1)} %pad_add_fusion.2.refs_0_, bf16[96,5248]{1,0:T(8,128)(2,1)} %collective-permute-done.4.refs_1_, bf16[96,5248]{1,0:T(8,128)(2,1)} %collective-permute-done.14.refs_2_, bf16[96,5248]{1,0:T(8,128)(2,1)} %collective-permute-done.15.refs_3_, ...), custom_call_target="tpu_custom_call", output_to_operand_aliasing={{}: (6, {})} | custom-call | flops 3221225472 | bytes 12812288 | tf_op jit(solution)/shard_map/pallas_call | solution.py:122
  124.1 0.0 collective-permute-done.13.refs_1_
  124.1 6.2 %shard_map.50.refs_6_ = bf16[1536,512]{1,0:T(8,128)(2,1)} custom-call(s32[4]{0:T(128)S(1)} %pad_add_fusion.1.refs_0_, bf16[96,5248]{1,0:T(8,128)(2,1)} %collective-permute-done.13.refs_1_, bf16[96,5248]{1,0:T(8,128)(2,1)} %collective-permute-done.1.refs_2_, bf16[96,5248]{1,0:T(8,128)(2,1)S(1)} %collective-permute-done.10.refs_3_, ...), custom_call_target="tpu_custom_call", output_to_operand_aliasing={{}: (6, {})} | custom-call | flops 3221225472 | bytes 12812288 | tf_op jit(solution)/shard_map/pallas_call | solution.py:122
  130.3 0.0 collective-permute-done.2.refs_1_
  130.3 0.0 collective-permute-done.5.refs_2_
  130.3 0.0 collective-permute-done.11.refs_4_
  130.3 5.3 %shard_map.51 = bf16[1536,512]{1,0:T(8,128)(2,1)} custom-call(s32[4]{0:T(128)S(1)} %pad_add_fusion.refs_0_, bf16[96,5248]{1,0:T(8,128)(2,1)} %collective-permute-done.2.refs_1_, bf16[96,5248]{1,0:T(8,128)(2,1)} %collective-permute-done.5.refs_2_, bf16[48,5248]{1,0:T(8,128)(2,1)S(1)} %collective-permute-done.9.refs_3_, ...), custom_call_target="tpu_custom_call", output_to_operand_aliasing={{}: (6, {})} | custom-call | flops 2415919104 | bytes 11706368 | tf_op jit(solution)/shard_map/pallas_call | solution.py:122
  (14 shorter events, 0.1 us)
Async XLA Ops:
  6.5 93.7 %all-gather.2.cloned.1.call-start = ((), (), s32[]{:S(2)}) async-start(), calls=%async_computation | async-start | bytes 9437184 | tf_op jit(solution)/shard_map/all_gather | solution.py:178
  6.5 2.4 %copy-start.6 = (s32[96,64]{0,1:T(8,128)S(1)}, s32[96,64]{0,1:T(8,128)}, u32[]{:S(2)}) copy-start(s32[96,64]{0,1:T(8,128)} %param.6) | copy-start | bytes 73732
  13.0 87.2 %copy-start.2 = (bf16[96,5248]{1,0:T(8,128)(2,1)S(1)}, bf16[96,5248]{1,0:T(8,128)(2,1)}, u32[]{:S(2)}) copy-start(bf16[96,5248]{1,0:T(8,128)(2,1)} %shard_map.46.refs_1_) | copy-start | bytes 3022852
  13.0 25.2 %collective-permute-start.6 = (bf16[96,5248]{1,0:T(8,128)(2,1)}, bf16[96,5248]{1,0:T(8,128)(2,1)S(1)}, u32[]{:S(2)}, u32[]{:S(2)}) collective-permute-start(bf16[96,5248]{1,0:T(8,128)(2,1)} %shard_map.46.refs_1_), channel_id=1, source_target_pairs={{0,12},{1,13},{2,14},{3,15},{4,0},{5,1},{6,2},{7,3},{8,4},{9,5},{1... | collective-permute-start | bytes 3022856 | tf_op jit(solution)/shard_map/ppermute | solution.py:181
  15.9 28.0 %collective-permute-start.3 = (bf16[96,5248]{1,0:T(8,128)(2,1)}, bf16[96,5248]{1,0:T(8,128)(2,1)}, u32[]{:S(2)}, u32[]{:S(2)}) collective-permute-start(bf16[96,5248]{1,0:T(8,128)(2,1)} %shard_map.46.refs_1_), channel_id=1, source_target_pairs={{0,4},{1,5},{2,6},{3,7},{4,8},{5,9},{6,10},{7,11},{8,12},{9,13},{1... | collective-permute-start | bytes 3022856 | tf_op jit(solution)/shard_map/ppermute | solution.py:181
  15.9 29.5 %collective-permute-start = (bf16[96,5248]{1,0:T(8,128)(2,1)}, bf16[96,5248]{1,0:T(8,128)(2,1)}, u32[]{:S(2)}, u32[]{:S(2)}) collective-permute-start(bf16[96,5248]{1,0:T(8,128)(2,1)} %shard_map.46.refs_1_), channel_id=1, source_target_pairs={{0,1},{1,2},{2,3},{3,0},{4,5},{5,6},{6,7},{7,4},{8,9},{9,10},{10,1... | collective-permute-start | bytes 3022856 | tf_op jit(solution)/shard_map/ppermute | solution.py:181
  38.2 25.5 %collective-permute-start.7 = (bf16[96,5248]{1,0:T(8,128)(2,1)S(1)}, bf16[96,5248]{1,0:T(8,128)(2,1)}, u32[]{:S(2)}, u32[]{:S(2)}) collective-permute-start(bf16[96,5248]{1,0:T(8,128)(2,1)S(1)} %collective-permute-done.6.refs_4_), channel_id=1, source_target_pairs={{0,3},{1,0},{2,1},{3,2},{4,7},{5,4},{6,5},{7,6},{8,11},{9,8},{10,9... | collective-permute-start | bytes 3022856 | tf_op jit(solution)/shard_map/ppermute | solution.py:181
  42.5 1.0 copy-start.3
  43.5 34.0 %collective-permute-start.12 = (bf16[96,5248]{1,0:T(8,128)(2,1)}, bf16[96,5248]{1,0:T(8,128)(2,1)}, u32[]{:S(2)}, u32[]{:S(2)}) collective-permute-start(bf16[96,5248]{1,0:T(8,128)(2,1)} %shard_map.46.refs_1_), channel_id=1, source_target_pairs={{0,3},{1,0},{2,1},{3,2},{4,7},{5,4},{6,5},{7,6},{8,11},{9,8},{10,9... | collective-permute-start | bytes 3022856 | tf_op jit(solution)/shard_map/ppermute | solution.py:181
  43.9 33.8 %collective-permute-start.4 = (bf16[96,5248]{1,0:T(8,128)(2,1)}, bf16[96,5248]{1,0:T(8,128)(2,1)}, u32[]{:S(2)}, u32[]{:S(2)}) collective-permute-start(bf16[96,5248]{1,0:T(8,128)(2,1)} %collective-permute-done.3.refs_2_), channel_id=1, source_target_pairs={{0,4},{1,5},{2,6},{3,7},{4,8},{5,9},{6,10},{7,11},{8,12},{9,13},{1... | collective-permute-start | bytes 3022856 | tf_op jit(solution)/shard_map/ppermute | solution.py:181
  45.4 35.1 %collective-permute-start.1 = (bf16[96,5248]{1,0:T(8,128)(2,1)}, bf16[96,5248]{1,0:T(8,128)(2,1)}, u32[]{:S(2)}, u32[]{:S(2)}) collective-permute-start(bf16[96,5248]{1,0:T(8,128)(2,1)} %collective-permute-done.refs_3_), channel_id=1, source_target_pairs={{0,1},{1,2},{2,3},{3,0},{4,5},{5,6},{6,7},{7,4},{8,9},{9,10},{10,1... | collective-permute-start | bytes 3022856 | tf_op jit(solution)/shard_map/ppermute | solution.py:181
  63.7 17.9 %collective-permute-start.10 = (bf16[96,5248]{1,0:T(8,128)(2,1)}, bf16[96,5248]{1,0:T(8,128)(2,1)S(1)}, u32[]{:S(2)}, u32[]{:S(2)}) collective-permute-start(bf16[96,5248]{1,0:T(8,128)(2,1)} %collective-permute-done.7.refs_4_), channel_id=1, source_target_pairs={{0,12},{1,13},{2,14},{3,15},{4,0},{5,1},{6,2},{7,3},{8,4},{9,5},{1... | collective-permute-start | bytes 3022856 | tf_op jit(solution)/shard_map/ppermute | solution.py:181
  67.5 31.5 %collective-permute-start.8 = (bf16[96,5248]{1,0:T(8,128)(2,1)}, bf16[96,5248]{1,0:T(8,128)(2,1)S(1)}, u32[]{:S(2)}, u32[]{:S(2)}) collective-permute-start(bf16[96,5248]{1,0:T(8,128)(2,1)} %collective-permute-done.7.refs_4_), channel_id=1, source_target_pairs={{0,3},{1,0},{2,1},{3,2},{4,7},{5,4},{6,5},{7,6},{8,11},{9,8},{10,9... | collective-permute-start | bytes 3022856 | tf_op jit(solution)/shard_map/ppermute | solution.py:181
  77.5 34.8 %collective-permute-start.14 = (bf16[96,5248]{1,0:T(8,128)(2,1)}, bf16[96,5248]{1,0:T(8,128)(2,1)}, u32[]{:S(2)}, u32[]{:S(2)}) collective-permute-start(bf16[96,5248]{1,0:T(8,128)(2,1)} %collective-permute-done.3.refs_2_), channel_id=1, source_target_pairs={{0,1},{1,2},{2,3},{3,0},{4,5},{5,6},{6,7},{7,4},{8,9},{9,10},{10,1... | collective-permute-start | bytes 3022856 | tf_op jit(solution)/shard_map/ppermute | solution.py:181
  77.7 38.4 %collective-permute-start.15 = (bf16[96,5248]{1,0:T(8,128)(2,1)}, bf16[96,5248]{1,0:T(8,128)(2,1)}, u32[]{:S(2)}, u32[]{:S(2)}) collective-permute-start(bf16[96,5248]{1,0:T(8,128)(2,1)} %collective-permute-done.refs_3_), channel_id=1, source_target_pairs={{0,12},{1,13},{2,14},{3,15},{4,0},{5,1},{6,2},{7,3},{8,4},{9,5},{1... | collective-permute-start | bytes 3022856 | tf_op jit(solution)/shard_map/ppermute | solution.py:181
  80.4 43.7 %collective-permute-start.13 = (bf16[96,5248]{1,0:T(8,128)(2,1)}, bf16[96,5248]{1,0:T(8,128)(2,1)}, u32[]{:S(2)}, u32[]{:S(2)}) collective-permute-start(bf16[96,5248]{1,0:T(8,128)(2,1)} %collective-permute-done.12.refs_5_), channel_id=1, source_target_pairs={{0,4},{1,5},{2,6},{3,7},{4,8},{5,9},{6,10},{7,11},{8,12},{9,13},{1... | collective-permute-start | bytes 3022856 | tf_op jit(solution)/shard_map/ppermute | solution.py:181
  81.6 48.7 %collective-permute-start.2 = (bf16[96,5248]{1,0:T(8,128)(2,1)}, bf16[96,5248]{1,0:T(8,128)(2,1)}, u32[]{:S(2)}, u32[]{:S(2)}) collective-permute-start(bf16[96,5248]{1,0:T(8,128)(2,1)} %collective-permute-done.1.refs_2_), channel_id=1, source_target_pairs={{0,4},{1,5},{2,6},{3,7},{4,8},{5,9},{6,10},{7,11},{8,12},{9,13},{1... | collective-permute-start | bytes 3022856 | tf_op jit(solution)/shard_map/ppermute | solution.py:181
  99.1 31.2 %collective-permute-start.5 = (bf16[96,5248]{1,0:T(8,128)(2,1)}, bf16[96,5248]{1,0:T(8,128)(2,1)}, u32[]{:S(2)}, u32[]{:S(2)}) collective-permute-start(bf16[96,5248]{1,0:T(8,128)(2,1)} %collective-permute-done.4.refs_1_), channel_id=1, source_target_pairs={{0,1},{1,2},{2,3},{3,0},{4,5},{5,6},{6,7},{7,4},{8,9},{9,10},{10,1... | collective-permute-start | bytes 3022856 | tf_op jit(solution)/shard_map/ppermute | solution.py:181
  100.2 3.4 %copy-start = (bf16[8192,512]{1,0:T(8,128)(2,1)S(1)}, bf16[8192,512]{1,0:T(8,128)(2,1)}, u32[]{:S(2)}) copy-start(bf16[8192,512]{1,0:T(8,128)(2,1)} %all-gather.2.cloned.1.call-done.refs_6_.refs_5_) | copy-start | bytes 25165828
  103.6 1.2 copy-start.4
  104.8 7.4 %copy-start.5 = (bf16[48,5248]{1,0:T(8,128)(2,1)S(1)}, bf16[48,5248]{1,0:T(8,128)(2,1)}, u32[]{:S(2)}) copy-start(bf16[48,5248]{1,0:T(8,128)(2,1)} %slice.9) | copy-start | bytes 1511428
  104.8 12.5 %copy-start.1 = (bf16[8192,512]{1,0:T(8,128)(2,1)S(1)}, bf16[8192,512]{1,0:T(8,128)(2,1)}, u32[]{:S(2)}) copy-start(bf16[8192,512]{1,0:T(8,128)(2,1)} %all-gather.2.cloned.1.call-done.refs_6_.refs_5_) | copy-start | bytes 25165828
  112.3 18.0 %collective-permute-start.11 = (bf16[48,5248]{1,0:T(8,128)(2,1)S(1)}, bf16[48,5248]{1,0:T(8,128)(2,1)S(1)}, u32[]{:S(2)}, u32[]{:S(2)}) collective-permute-start(bf16[48,5248]{1,0:T(8,128)(2,1)S(1)} %copy-done.5), channel_id=1, source_target_pairs={{0,3},{1,0},{2,1},{3,2},{4,7},{5,4},{6,5},{7,6},{8,11},{9,8},{10,9... | collective-permute-start | bytes 1511432 | tf_op jit(solution)/shard_map/ppermute | solution.py:181
  116.0 14.3 %collective-permute-start.9 = (bf16[48,5248]{1,0:T(8,128)(2,1)S(1)}, bf16[48,5248]{1,0:T(8,128)(2,1)S(1)}, u32[]{:S(2)}, u32[]{:S(2)}) collective-permute-start(bf16[48,5248]{1,0:T(8,128)(2,1)S(1)} %slice.8), channel_id=1, source_target_pairs={{0,12},{1,13},{2,14},{3,15},{4,0},{5,1},{6,2},{7,3},{8,4},{9,5},{1... | collective-permute-start | bytes 1511432 | tf_op jit(solution)/shard_map/ppermute | solution.py:181
Sparse Core Ops, SparseCore 0:
  9.1 52.1 all-gather.1

commit v2 on v1

v2 whole, which is shorter than its diff:
```python
import functools

import jax
import jax.numpy as jnp
from jax import lax
from jax.experimental import pallas as pl
from jax.experimental.pallas import tpu as pltpu
from jax.sharding import PartitionSpec as P

TILE = 128
KT = 64
SLOTS = 40
FOLD = KT - SLOTS
WIDE = (SLOTS + 1) * TILE
BF = jnp.bfloat16


def pack_kernel(mask_ref, amps_ref, *outs):
    rows = amps_ref.shape[0]
    mask = mask_ref[...].T
    tile = lax.broadcasted_iota(jnp.int32, mask.shape, 1)
    count = jnp.sum(mask, axis=1, keepdims=True)
    low = jnp.min(jnp.where(mask > 0, tile, KT), axis=1, keepdims=True)
    high = jnp.max(jnp.where(mask > 0, tile, -1), axis=1, keepdims=True)
    end = jnp.min(jnp.where(mask > 0, KT, tile), axis=1, keepdims=True)
    wraps = high - low + 1 > count
    alpha = jnp.where(wraps, 0, jnp.minimum(low, FOLD))
    beta = jnp.where(wraps, end, SLOTS)
    first = jnp.where(wraps, end + KT - count, low)
    last = jnp.where(wraps, KT, high + 1)
    wide = lambda v: jnp.broadcast_to(v.astype(jnp.float32), (rows, TILE)).astype(BF)
    code = wide(jnp.where(wraps, -end, alpha))
    alpha, beta, first, last = wide(alpha), wide(beta), wide(first), wide(last)
    zero = jnp.zeros((rows, TILE), BF)

    def tile_of(t):
        return amps_ref[:, t * TILE : (t + 1) * TILE]

    def put(j, value):
        row = 0
        for out in outs:
            n = out.shape[0]
            out[:, j * TILE : (j + 1) * TILE] = value[row : row + n]
            row += n

    for j in range(SLOTS):
        value = jnp.where((first <= j) & (j < last), tile_of(j), zero)
        value = jnp.where((beta < SLOTS) & (j < beta), tile_of(j), value)
        far = jnp.where((first <= j + FOLD) & (j + FOLD < last), tile_of(j + FOLD), zero)
        value = jnp.where(beta <= j, far, value)
        if j < FOLD:
            up = jnp.where((first <= j + SLOTS) & (j + SLOTS < last), tile_of(j + SLOTS), zero)
            value = jnp.where(j < alpha, up, value)
        put(j, value)
    put(SLOTS, code)


def ints_kernel(mask_ref, ints_ref, kept_ref):
    for i in range(ints_ref.shape[0] // TILE):
        for j in range(ints_ref.shape[1] // TILE):
            at = (slice(i * TILE, (i + 1) * TILE), slice(j * TILE, (j + 1) * TILE))
            keep = jnp.full((TILE, TILE), mask_ref[j, i].astype(jnp.float32), jnp.float32).astype(BF)
            kept_ref[at] = ints_ref[at] * keep


def mm_kernel(spots, chunks, offs, *refs):
    n = len(spots)
    amps, ints = refs[:n], refs[n]
    out, land, wide, done, amp_sems, out_sems = refs[-6:]
    rows = amps[0].shape[0]
    place = [pl.ds(i * rows, rows) for i in range(n)]
    loads = [pltpu.make_async_copy(amps[i], land.at[place[i]], amp_sems.at[i]) for i in range(n)]
    stores = [
        pltpu.make_async_copy(done.at[place[i]], out.at[pl.ds(pl.multiple_of(offs[spots[i]], 16), rows)], out_sems.at[i])
        for i in range(n)
    ]
    for load in loads:
        load.start()

    def fill(i):
        here = slice(i * rows, (i + 1) * rows)
        code = land[here, SLOTS * TILE :]
        zero = jnp.zeros((rows, TILE), BF)
        alpha = jnp.where(code < 0, zero, code)
        beta = jnp.where(code < 0, zero - code, zero + SLOTS)

        def slot(j):
            return land[here, j * TILE : (j + 1) * TILE]

        for t in range(KT):
            if t < FOLD:
                v = jnp.where((alpha <= t) & (t < beta), slot(t), zero)
            elif t < SLOTS:
                v = jnp.where(t < beta, slot(t), zero)
                v = jnp.where(beta <= t - FOLD, slot(t - FOLD), v)
            else:
                v = jnp.where(t - SLOTS < alpha, slot(t - SLOTS), zero)
                v = jnp.where(beta <= t - FOLD, slot(t - FOLD), v)
            wide[here, t * TILE : (t + 1) * TILE] = v

    first = 0
    for size in chunks:
        for i in range(first, first + size):
            loads[i].wait()
            fill(i)
        here = slice(first * rows, (first + size) * rows)
        done[here, :] = jnp.dot(wide[here, :], ints[...], preferred_element_type=jnp.float32).astype(BF)
        for i in range(first, first + size):
            stores[i].start()
        first += size
    for store in stores:
        store.wait()


def multiply(amps, spots, chunks, offs, ints, out, out_rows):
    rows = sum(v.shape[0] for v in amps)
    cols = ints.shape[1]
    anywhere = pl.BlockSpec(memory_space=pl.ANY)
    in_specs = [pl.BlockSpec(memory_space=pltpu.SMEM)] + [anywhere] * len(amps) + [pl.BlockSpec(memory_space=pltpu.VMEM)]
    args = [offs] + list(amps) + [ints]
    alias = {}
    if out is not None:
        in_specs.append(anywhere)
        alias = {len(args): 0}
        args.append(out)
    return pl.pallas_call(
        functools.partial(mm_kernel, tuple(spots), tuple(chunks)),
        out_shape=jax.ShapeDtypeStruct((out_rows, cols), BF),
        in_specs=in_specs,
        out_specs=anywhere,
        scratch_shapes=[
            pltpu.VMEM((rows, WIDE), BF),
            pltpu.VMEM((rows, KT * TILE), BF),
            pltpu.VMEM((rows, cols), BF),
            pltpu.SemaphoreType.DMA((len(amps),)),
            pltpu.SemaphoreType.DMA((len(amps),)),
        ],
        input_output_aliases=alias,
        compiler_params=pltpu.CompilerParams(vmem_limit_bytes=16 * 2**20),
        cost_estimate=pl.CostEstimate(
            flops=2 * rows * KT * TILE * cols,
            bytes_accessed=2 * (rows * WIDE + KT * TILE * cols + rows * cols),
            transcendentals=0,
        ),
    )(*args)


def pack(mask, amps):
    rows = amps.shape[0]
    sizes = [rows]
    return pl.pallas_call(
        pack_kernel,
        out_shape=[jax.ShapeDtypeStruct((n, WIDE), BF) for n in sizes],
    )(mask.T, amps)


def mask_ints(mask, ints):
    return pl.pallas_call(
        ints_kernel,
        out_shape=jax.ShapeDtypeStruct(ints.shape, ints.dtype),
        in_specs=[pl.BlockSpec(memory_space=pltpu.SMEM), pl.BlockSpec(memory_space=pltpu.VMEM)],
        out_specs=pl.BlockSpec(memory_space=pltpu.VMEM),
    )(mask.T, ints)


def moves(n, n_row):
    def shift(dx, dz):
        pairs = []
        for r in range(n_row):
            s = 1 - 2 * (r % 2)
            for x in range(n):
                for z in range(n):
                    pairs.append(((r * n + x) * n + z, (r * n + (x + s * dx) % n) * n + (z + s * dz) % n))
        return pairs

    return shift(1, 0), shift(0, 1)


def join_kernel(offs, *refs):
    blocks, out, sems = refs[:-2], refs[-2], refs[-1]
    copies = []
    for i, block in enumerate(blocks):
        rows = block.shape[0]
        there = pl.ds(pl.multiple_of(offs[i] * rows, rows), rows)
        copies.append(pltpu.make_async_copy(block, out.at[there], sems.at[i]))
    for copy in copies:
        copy.start()
    for copy in copies:
        copy.wait()


def join(blocks, places):
    rows, cols = blocks[0].shape
    return pl.pallas_call(
        join_kernel,
        out_shape=jax.ShapeDtypeStruct((rows * len(blocks), cols), BF),
        in_specs=[pl.BlockSpec(memory_space=pltpu.SMEM)] + [pl.BlockSpec(memory_space=pl.ANY)] * len(blocks),
        out_specs=pl.BlockSpec(memory_space=pltpu.VMEM),
        scratch_shapes=[pltpu.SemaphoreType.DMA((len(blocks),))],
        compiler_params=pltpu.CompilerParams(vmem_limit_bytes=16 * 2**20),
    )(places.astype(jnp.int32), *blocks)


def after(value, *first):
    return lax.optimization_barrier((value, *first))[0]


def on_device(amplitudes, integrals, amplitude_mask, integral_mask):
    dev_rows = amplitudes.shape[0]
    own = pack(amplitude_mask, amplitudes)[0]
    kept_ints = mask_ints(integral_mask, integrals)
    row = lax.axis_index("row")
    core, y = row % 2, row // 2
    sign = 1 - 2 * core
    by_y = lambda v: lax.ppermute(v, "row", [(r, (r + (2 if r % 2 == 0 else -2)) % 8) for r in range(8)])
    swap = lambda v: lax.ppermute(v, "row", [(r, r ^ 1) for r in range(8)])
    step = jnp.arange(4)
    along_x, along_z = moves(4, 8)
    by_x = lambda v: lax.ppermute(v, ("row", "col"), along_x)
    by_z = lambda v: lax.ppermute(v, ("row", "col"), along_z)
    me = lax.axis_index("col")
    x, z = me // 4, me % 4
    spot = jnp.arange(16)
    offs = ((x - sign * (spot // 4) + 4) % 4 * 4 + (z - sign * (spot % 4) + 4) % 4) * dev_rows
    offs = offs.astype(jnp.int32)
    total = 16 * dev_rows

    b10, b01 = by_x(own), by_z(own)
    i0 = kept_ints
    i1, s0 = by_y(i0), swap(i0)
    b20, b02, b11 = by_x(after(b10, b01)), by_z(after(b01, b10)), by_x(b01)
    i2, s1 = by_y(after(i1, s0, b10, b01)), swap(i1)
    b21, b30, b03, b12 = by_z(after(b20, b02)), by_x(after(b20, b02)), by_z(b02), by_x(after(b02, b11))
    i3, s2 = by_y(after(i2, s1, b20, b02)), swap(i2)
    s3 = swap(after(i3, s2))
    b22 = by_z(after(b21, b11))
    places = jnp.concatenate([(y - sign * step + 4) % 4 * 2 + core, (y + sign * step + 4) % 4 * 2 + 1 - core])
    ints = join([i0, i1, i2, i3, s0, s1, s2, s3], places)

    b13, b31 = by_x(after(b03, b12)), by_z(after(b30, b03))
    b32, b23 = by_x(after(b22, b12)), by_z(after(b22, b03))
    b33 = by_z(b32)
    out = multiply([own, b10, b01, b20, b02], [0, 4, 1, 8, 2], [2, 3], offs, ints, None, total)
    out = multiply([b11, b21, b30, b03], [5, 9, 12, 3], [2, 2], offs, ints, out, total)
    out = multiply([b12, b22, b13, b31], [6, 10, 7, 13], [2, 2], offs, ints, out, total)
    out = multiply([b32, b23], [14, 11], [2], offs, ints, out, total)
    return multiply([b33], [15], [1], offs, ints, out, total)


def solution(mesh):
    in_specs = (P(("row", "col"), None), P("row", "col"), P(("row", "col"), None), P("row", "col"))
    out_specs = P("row", "col")
    return jax.shard_map(
        on_device, mesh=mesh, in_specs=in_specs, out_specs=out_specs, check_vma=False
    )
```

time: 143 us -> 124 us (0.87)
  the two profiles are of different devices: /device:TPU:0 before, /device:TPU:34 now
where the time goes in v2:
time: 124 us; the launch traced here: 122 us
  waiting for transfers between devices  49.7 us (40%)
  Pallas kernels  40.2 us (32%)
  starting transfers between devices  23 us (19%)
  local copies, waits for them, and re-layouts  8.52 us (7%)
    pallas_call x5, Pallas kernels, multiply(): pl.pallas_call(functools.partial(mm_kernel, tuple(spots), tuple(chunks)),...  32 us
    ppermute x8, waiting for transfers between devices, on_device(): by_z = lambda v: lax.ppermute(v, ('row', 'col'), along_z)  19.1 us
    ppermute x7, waiting for transfers between devices, on_device(): by_x = lambda v: lax.ppermute(v, ('row', 'col'), along_x)  18 us
    ppermute x3, waiting for transfers between devices, on_device(): lax.ppermute(v, 'row', [(r, (r + (2 if r % 2 == 0 else -2)) % 8) for r in...  12.6 us
    ppermute x8, starting transfers between devices, on_device(): by_z = lambda v: lax.ppermute(v, ('row', 'col'), along_z)  10.9 us
    ppermute x7, starting transfers between devices, on_device(): by_x = lambda v: lax.ppermute(v, ('row', 'col'), along_x)  10.1 us
    unnamed x24, local copies, waits for them, and re-layouts  8.52 us
    pallas_call x1, Pallas kernels, pack(): pl.pallas_call(pack_kernel, out_shape=[jax.ShapeDtypeStruct((n, WIDE), BF...  3.4 us
  transfers between devices with their start and end apart: 22, of which 13 were waited for; matrix products, arithmetic and copies ran while one was open for 0% of the time, Pallas kernels for 28%

profile of v2, /device:TPU:34, one launch (start us, length us, event | category | flops | bytes accessed | tf_op | source)
XLA Modules:
  0.0 121.9 jit_solution(10572951903144246025)
XLA Ops:
  0.0 3.4 %shard_map.46.refs_0_ = bf16[96,5248]{1,0:T(8,128)(2,1)} custom-call(s32[64,96]{1,0:T(8,128)} %bitcast.2, bf16[96,8192]{1,0:T(8,128)(2,1)} %amps_ref.1), custom_call_target="tpu_custom_call" | custom-call | tf_op jit(solution)/shard_map/pallas_call | solution.py:151
  3.4 1.9 %collective-permute-start.1 = (bf16[96,5248]{1,0:T(8,128)(2,1)}, bf16[96,5248]{1,0:T(8,128)(2,1)}, u32[]{:S(2)}, u32[]{:S(2)}) collective-permute-start(bf16[96,5248]{1,0:T(8,128)(2,1)} %shard_map.46.refs_0_), channel_id=1, source_target_pairs={{0,1},{1,2},{2,3},{3,0},{4,5},{5,6},{6,7},{7,4},{8,9},{9,10},{10,1... | collective-permute-start | bytes 3022856 | tf_op jit(solution)/shard_map/ppermute | solution.py:220
  5.3 1.5 %collective-permute-start = (bf16[96,5248]{1,0:T(8,128)(2,1)}, bf16[96,5248]{1,0:T(8,128)(2,1)}, u32[]{:S(2)}, u32[]{:S(2)}) collective-permute-start(bf16[96,5248]{1,0:T(8,128)(2,1)} %shard_map.46.refs_0_), channel_id=1, source_target_pairs={{0,4},{1,5},{2,6},{3,7},{4,8},{5,9},{6,10},{7,11},{8,12},{9,13},{1... | collective-permute-start | bytes 3022856 | tf_op jit(solution)/shard_map/ppermute | solution.py:219
  6.8 2.4 %shard_map.47.refs_0_ = bf16[1024,512]{1,0:T(8,128)(2,1)} custom-call(s32[4,8]{1,0:T(4,128)} %bitcast.3, bf16[1024,512]{1,0:T(8,128)(2,1)} %ints_ref.1), custom_call_target="tpu_custom_call" | custom-call | tf_op jit(solution)/shard_map/pallas_call | solution.py:158
  9.2 1.6 %collective-permute-start.10 = (bf16[1024,512]{1,0:T(8,128)(2,1)}, bf16[1024,512]{1,0:T(8,128)(2,1)S(1)}, u32[]{:S(2)}, u32[]{:S(2)}) collective-permute-start(bf16[1024,512]{1,0:T(8,128)(2,1)} %shard_map.47.refs_0_), channel_id=1, source_target_pairs={{0,32},{16,112},{32,64},{48,16},{64,96},{80,48},{96,0},{112,80},{1... | collective-permute-start | bytes 3145736 | tf_op jit(solution)/shard_map/ppermute | solution.py:215
  10.8 7.3 %collective-permute-done.1.refs_2_ = bf16[96,5248]{1,0:T(8,128)(2,1)} collective-permute-done((bf16[96,5248]{1,0:T(8,128)(2,1)}, bf16[96,5248]{1,0:T(8,128)(2,1)}, u32[]{:S(2)}, u32[]{:S(2)}) %collective-permute-start.1) | collective-permute-done | bytes 1007648 | tf_op jit(solution)/shard_map/ppermute | solution.py:220
  18.1 1.9 %collective-permute-done.refs_1_ = bf16[96,5248]{1,0:T(8,128)(2,1)} collective-permute-done((bf16[96,5248]{1,0:T(8,128)(2,1)}, bf16[96,5248]{1,0:T(8,128)(2,1)}, u32[]{:S(2)}, u32[]{:S(2)}) %collective-permute-start) | collective-permute-done | bytes 1007648 | tf_op jit(solution)/shard_map/ppermute | solution.py:219
  20.0 1.6 %collective-permute-start.3 = (bf16[96,5248]{1,0:T(8,128)(2,1)}, bf16[96,5248]{1,0:T(8,128)(2,1)}, u32[]{:S(2)}, u32[]{:S(2)}) collective-permute-start(bf16[96,5248]{1,0:T(8,128)(2,1)} %collective-permute-done.1.refs_2_), channel_id=1, source_target_pairs={{0,1},{1,2},{2,3},{3,0},{4,5},{5,6},{6,7},{7,4},{8,9},{9,10},{10,1... | collective-permute-start | bytes 3022856 | tf_op jit(solution)/shard_map/ppermute | solution.py:220
  21.6 1.5 %collective-permute-start.2 = (bf16[96,5248]{1,0:T(8,128)(2,1)}, bf16[96,5248]{1,0:T(8,128)(2,1)}, u32[]{:S(2)}, u32[]{:S(2)}) collective-permute-start(bf16[96,5248]{1,0:T(8,128)(2,1)} %collective-permute-done.refs_1_), channel_id=1, source_target_pairs={{0,4},{1,5},{2,6},{3,7},{4,8},{5,9},{6,10},{7,11},{8,12},{9,13},{1... | collective-permute-start | bytes 3022856 | tf_op jit(solution)/shard_map/ppermute | solution.py:219
  23.1 2.3 %collective-permute-done.10.refs_1_ = bf16[1024,512]{1,0:T(8,128)(2,1)S(1)} collective-permute-done((bf16[1024,512]{1,0:T(8,128)(2,1)}, bf16[1024,512]{1,0:T(8,128)(2,1)S(1)}, u32[]{:S(2)}, u32[]{:S(2)}) %collective-permute-start.10) | collective-permute-done | bytes 1048608 | tf_op jit(solution)/shard_map/ppermute | solution.py:215
  25.4 0.4 collective-permute-start.12
  25.8 1.2 collective-permute-start.5
  27.0 7.7 %collective-permute-done.3.refs_4_ = bf16[96,5248]{1,0:T(8,128)(2,1)} collective-permute-done((bf16[96,5248]{1,0:T(8,128)(2,1)}, bf16[96,5248]{1,0:T(8,128)(2,1)}, u32[]{:S(2)}, u32[]{:S(2)}) %collective-permute-start.3) | collective-permute-done | bytes 1007648 | tf_op jit(solution)/shard_map/ppermute | solution.py:220
  34.7 1.6 %collective-permute-done.2.refs_3_ = bf16[96,5248]{1,0:T(8,128)(2,1)} collective-permute-done((bf16[96,5248]{1,0:T(8,128)(2,1)}, bf16[96,5248]{1,0:T(8,128)(2,1)}, u32[]{:S(2)}, u32[]{:S(2)}) %collective-permute-start.2) | collective-permute-done | bytes 1007648 | tf_op jit(solution)/shard_map/ppermute | solution.py:219
  36.3 0.0 collective-permute-start.4
  36.3 5.1 %collective-permute-done.12.refs_2_ = bf16[1024,512]{1,0:T(8,128)(2,1)S(1)} collective-permute-done((bf16[1024,512]{1,0:T(8,128)(2,1)S(1)}, bf16[1024,512]{1,0:T(8,128)(2,1)S(1)}, u32[]{:S(2)}, u32[]{:S(2)}) %collective-permute-start.12) | collective-permute-done | bytes 1048608 | tf_op jit(solution)/shard_map/ppermute | solution.py:215
  41.4 1.0 copy-done.2
  42.4 4.6 %collective-permute-done.5.refs_0_ = bf16[96,5248]{1,0:T(8,128)(2,1)S(1)} collective-permute-done((bf16[96,5248]{1,0:T(8,128)(2,1)}, bf16[96,5248]{1,0:T(8,128)(2,1)S(1)}, u32[]{:S(2)}, u32[]{:S(2)}) %collective-permute-start.5) | collective-permute-done | bytes 1007648 | tf_op jit(solution)/shard_map/ppermute | solution.py:219
  47.0 1.0 copy-done.6
  48.0 1.5 %collective-permute-start.7 = (bf16[96,5248]{1,0:T(8,128)(2,1)}, bf16[96,5248]{1,0:T(8,128)(2,1)S(1)}, u32[]{:S(2)}, u32[]{:S(2)}) collective-permute-start(bf16[96,5248]{1,0:T(8,128)(2,1)} %collective-permute-done.3.refs_4_), channel_id=1, source_target_pairs={{0,4},{1,5},{2,6},{3,7},{4,8},{5,9},{6,10},{7,11},{8,12},{9,13},{1... | collective-permute-start | bytes 3022856 | tf_op jit(solution)/shard_map/ppermute | solution.py:219
  49.4 1.4 %collective-permute-done.4.refs_1_ = bf16[96,5248]{1,0:T(8,128)(2,1)S(1)} collective-permute-done((bf16[96,5248]{1,0:T(8,128)(2,1)}, bf16[96,5248]{1,0:T(8,128)(2,1)S(1)}, u32[]{:S(2)}, u32[]{:S(2)}) %collective-permute-start.4) | collective-permute-done | bytes 1007648 | tf_op jit(solution)/shard_map/ppermute | solution.py:220
  50.9 0.0 collective-permute-start.6
  50.9 1.0 copy-done.8
  51.8 1.5 %collective-permute-start.20 = (bf16[96,5248]{1,0:T(8,128)(2,1)}, bf16[96,5248]{1,0:T(8,128)(2,1)}, u32[]{:S(2)}, u32[]{:S(2)}) collective-permute-start(bf16[96,5248]{1,0:T(8,128)(2,1)} %collective-permute-done.2.refs_3_), channel_id=1, source_target_pairs={{0,4},{1,5},{2,6},{3,7},{4,8},{5,9},{6,10},{7,11},{8,12},{9,13},{1... | collective-permute-start | bytes 3022856 | tf_op jit(solution)/shard_map/ppermute | solution.py:219
  53.3 5.2 %collective-permute-done.14.refs_3_ = bf16[1024,512]{1,0:T(8,128)(2,1)} collective-permute-done((bf16[1024,512]{1,0:T(8,128)(2,1)S(1)}, bf16[1024,512]{1,0:T(8,128)(2,1)}, u32[]{:S(2)}, u32[]{:S(2)}) %collective-permute-start.14) | collective-permute-done | bytes 1048608 | tf_op jit(solution)/shard_map/ppermute | solution.py:215
  58.5 1.6 %collective-permute-start.17 = (bf16[96,5248]{1,0:T(8,128)(2,1)}, bf16[96,5248]{1,0:T(8,128)(2,1)}, u32[]{:S(2)}, u32[]{:S(2)}) collective-permute-start(bf16[96,5248]{1,0:T(8,128)(2,1)} %collective-permute-done.3.refs_4_), channel_id=1, source_target_pairs={{0,1},{1,2},{2,3},{3,0},{4,5},{5,6},{6,7},{7,4},{8,9},{9,10},{10,1... | collective-permute-start | bytes 3022856 | tf_op jit(solution)/shard_map/ppermute | solution.py:220
  60.1 1.0 copy-done.4
  61.1 2.3 %collective-permute-done.7.refs_0_ = bf16[96,5248]{1,0:T(8,128)(2,1)S(1)} collective-permute-done((bf16[96,5248]{1,0:T(8,128)(2,1)}, bf16[96,5248]{1,0:T(8,128)(2,1)S(1)}, u32[]{:S(2)}, u32[]{:S(2)}) %collective-permute-start.7) | collective-permute-done | bytes 1007648 | tf_op jit(solution)/shard_map/ppermute | solution.py:219
  63.5 1.0 copy-done.10
  64.4 0.9 collective-permute-done.6.refs_1_
  65.3 1.5 %collective-permute-start.8 = (bf16[96,5248]{1,0:T(8,128)(2,1)}, bf16[96,5248]{1,0:T(8,128)(2,1)}, u32[]{:S(2)}, u32[]{:S(2)}) collective-permute-start(bf16[96,5248]{1,0:T(8,128)(2,1)} %collective-permute-done.6.refs_1_), channel_id=1, source_target_pairs={{0,4},{1,5},{2,6},{3,7},{4,8},{5,9},{6,10},{7,11},{8,12},{9,13},{1... | collective-permute-start | bytes 3022856 | tf_op jit(solution)/shard_map/ppermute | solution.py:219
  66.8 7.5 %collective-permute-done.20.refs_2_ = bf16[96,5248]{1,0:T(8,128)(2,1)} collective-permute-done((bf16[96,5248]{1,0:T(8,128)(2,1)}, bf16[96,5248]{1,0:T(8,128)(2,1)}, u32[]{:S(2)}, u32[]{:S(2)}) %collective-permute-start.20) | collective-permute-done | bytes 1007648 | tf_op jit(solution)/shard_map/ppermute | solution.py:219
  74.4 1.8 %collective-permute-done.17.refs_3_ = bf16[96,5248]{1,0:T(8,128)(2,1)} collective-permute-done((bf16[96,5248]{1,0:T(8,128)(2,1)}, bf16[96,5248]{1,0:T(8,128)(2,1)}, u32[]{:S(2)}, u32[]{:S(2)}) %collective-permute-start.17) | collective-permute-done | bytes 1007648 | tf_op jit(solution)/shard_map/ppermute | solution.py:220
  76.1 0.0 collective-permute-start.21
  76.1 1.5 %collective-permute-start.19 = (bf16[96,5248]{1,0:T(8,128)(2,1)}, bf16[96,5248]{1,0:T(8,128)(2,1)S(1)}, u32[]{:S(2)}, u32[]{:S(2)}) collective-permute-start(bf16[96,5248]{1,0:T(8,128)(2,1)} %collective-permute-done.17.refs_3_), channel_id=1, source_target_pairs={{0,4},{1,5},{2,6},{3,7},{4,8},{5,9},{6,10},{7,11},{8,12},{9,13},{1... | collective-permute-start | bytes 3022856 | tf_op jit(solution)/shard_map/ppermute | solution.py:219
  77.6 0.1 pad_add_fusion.offs
  77.7 1.8 %collective-permute-start.18 = (bf16[96,5248]{1,0:T(8,128)(2,1)}, bf16[96,5248]{1,0:T(8,128)(2,1)S(1)}, u32[]{:S(2)}, u32[]{:S(2)}) collective-permute-start(bf16[96,5248]{1,0:T(8,128)(2,1)} %collective-permute-done.6.refs_1_), channel_id=1, source_target_pairs={{0,1},{1,2},{2,3},{3,0},{4,5},{5,6},{6,7},{7,4},{8,9},{9,10},{10,1... | collective-permute-start | bytes 3022856 | tf_op jit(solution)/shard_map/ppermute | solution.py:220
  79.5 0.0 copy-start
  79.5 1.2 copy-done
  80.7 1.2 %copy-done.3 = bf16[1024,512]{1,0:T(8,128)(2,1)S(1)} copy-done((bf16[1024,512]{1,0:T(8,128)(2,1)S(1)}, bf16[1024,512]{1,0:T(8,128)(2,1)}, u32[]{:S(2)}) %copy-start.3) | copy-done | bytes 1048600
  82.0 1.2 %copy-done.5 = bf16[1024,512]{1,0:T(8,128)(2,1)S(1)} copy-done((bf16[1024,512]{1,0:T(8,128)(2,1)S(1)}, bf16[1024,512]{1,0:T(8,128)(2,1)}, u32[]{:S(2)}) %copy-start.5) | copy-done | bytes 1048600
  83.2 2.4 %shard_map.48.refs_5_.refs_4_.refs_2_.refs_1_ = bf16[8192,512]{1,0:T(8,128)(2,1)S(1)} custom-call(s32[8]{0:T(128)S(1)} %pad_add_fusion.offs, bf16[1024,512]{1,0:T(8,128)(2,1)S(1)} %copy-done, bf16[1024,512]{1,0:T(8,128)(2,1)S(1)} %collective-permute-done.10.refs_1_, bf16[1024,512]{1,0:T(8,128)(2,1)S(1)} %collective-permute-done.12.refs_2_, ...), custom_call_target="tpu_custom_call" | custom-call | tf_op jit(solution)/shard_map/pallas_call | solution.py:194
  85.7 3.9 %collective-permute-start.9 = (bf16[96,5248]{1,0:T(8,128)(2,1)}, bf16[96,5248]{1,0:T(8,128)(2,1)S(1)}, u32[]{:S(2)}, u32[]{:S(2)}) collective-permute-start(bf16[96,5248]{1,0:T(8,128)(2,1)} %collective-permute-done.8.refs_0_), channel_id=1, source_target_pairs={{0,1},{1,2},{2,3},{3,0},{4,5},{5,6},{6,7},{7,4},{8,9},{9,10},{10,1... | collective-permute-start | bytes 3022856 | tf_op jit(solution)/shard_map/ppermute | solution.py:220
  89.6 8.9 %shard_map.49.refs_5_ = bf16[1536,512]{1,0:T(8,128)(2,1)} custom-call(s32[16]{0:T(128)S(1)} %fusion.14.offs, bf16[96,5248]{1,0:T(8,128)(2,1)S(1)} %copy-done.1, bf16[96,5248]{1,0:T(8,128)(2,1)} %collective-permute-done.refs_1_, bf16[96,5248]{1,0:T(8,128)(2,1)} %collective-permute-done.1.refs_2_, bf16[96,5248]{1,0:T(8,128)(2,1)} %collective-permute-done.2.refs_3_, ...), custom_call_target="tpu_custom_call" | custom-call | flops 4026531840 | bytes 13918208 | tf_op jit(solution)/shard_map/pallas_call | solution.py:126
  98.5 7.2 %shard_map.50.refs_5_ = bf16[1536,512]{1,0:T(8,128)(2,1)} custom-call(s32[16]{0:T(128)S(1)} %fusion.14.offs, bf16[96,5248]{1,0:T(8,128)(2,1)S(1)} %copy-done.7, bf16[96,5248]{1,0:T(8,128)(2,1)S(1)} %copy-done.9, bf16[96,5248]{1,0:T(8,128)(2,1)} %collective-permute-done.20.refs_2_, ...), custom_call_target="tpu_custom_call", output_to_operand_aliasing={{}: (6, {})} | custom-call | flops 3221225472 | bytes 12812288 | tf_op jit(solution)/shard_map/pallas_call | solution.py:126
  105.7 7.7 %shard_map.51.refs_3_ = bf16[1536,512]{1,0:T(8,128)(2,1)} custom-call(s32[16]{0:T(128)S(1)} %fusion.14.offs, bf16[96,5248]{1,0:T(8,128)(2,1)S(1)} %copy-done.11, bf16[96,5248]{1,0:T(8,128)(2,1)} %collective-permute-done.6.refs_1_, bf16[96,5248]{1,0:T(8,128)(2,1)S(1)} %collective-permute-done.19.refs_2_, ...), custom_call_target="tpu_custom_call", output_to_operand_aliasing={{}: (6, {})} | custom-call | flops 3221225472 | bytes 12812288 | tf_op jit(solution)/shard_map/pallas_call | solution.py:126
  113.5 5.1 %shard_map.52.refs_2_ = bf16[1536,512]{1,0:T(8,128)(2,1)} custom-call(s32[16]{0:T(128)S(1)} %fusion.14.offs, bf16[96,5248]{1,0:T(8,128)(2,1)} %collective-permute-done.8.refs_0_, bf16[96,5248]{1,0:T(8,128)(2,1)S(1)} %collective-permute-done.18.refs_1_, ...), custom_call_target="tpu_custom_call", output_to_operand_aliasing={{}: (4, {})} | custom-call | flops 1610612736 | bytes 10600448 | tf_op jit(solution)/shard_map/pallas_call | solution.py:126
  118.6 3.1 %shard_map.53 = bf16[1536,512]{1,0:T(8,128)(2,1)} custom-call(s32[16]{0:T(128)S(1)} %fusion.14.offs, bf16[96,5248]{1,0:T(8,128)(2,1)S(1)} %collective-permute-done.9.refs_0_, bf16[8192,512]{1,0:T(8,128)(2,1)S(1)} %shard_map.48.refs_5_.refs_4_.refs_2_.refs_1_, bf16[1536,512]{1,0:T(8,128)(2,1)} %shard_map.52.refs_2_), custom_call_target="tpu_custom_call", output_to_operand_aliasing={{}: (3, {})} | custom-call | flops 805306368 | bytes 9494528 | tf_op jit(solution)/shard_map/pallas_call | solution.py:126
  (31 shorter events, 0.1 us)
Async XLA Ops:
  3.4 14.7 %collective-permute-start.1 = (bf16[96,5248]{1,0:T(8,128)(2,1)}, bf16[96,5248]{1,0:T(8,128)(2,1)}, u32[]{:S(2)}, u32[]{:S(2)}) collective-permute-start(bf16[96,5248]{1,0:T(8,128)(2,1)} %shard_map.46.refs_0_), channel_id=1, source_target_pairs={{0,1},{1,2},{2,3},{3,0},{4,5},{5,6},{6,7},{7,4},{8,9},{9,10},{10,1... | collective-permute-start | bytes 3022856 | tf_op jit(solution)/shard_map/ppermute | solution.py:220
  5.3 14.7 %collective-permute-start = (bf16[96,5248]{1,0:T(8,128)(2,1)}, bf16[96,5248]{1,0:T(8,128)(2,1)}, u32[]{:S(2)}, u32[]{:S(2)}) collective-permute-start(bf16[96,5248]{1,0:T(8,128)(2,1)} %shard_map.46.refs_0_), channel_id=1, source_target_pairs={{0,4},{1,5},{2,6},{3,7},{4,8},{5,9},{6,10},{7,11},{8,12},{9,13},{1... | collective-permute-start | bytes 3022856 | tf_op jit(solution)/shard_map/ppermute | solution.py:219
  9.2 16.2 %collective-permute-start.10 = (bf16[1024,512]{1,0:T(8,128)(2,1)}, bf16[1024,512]{1,0:T(8,128)(2,1)S(1)}, u32[]{:S(2)}, u32[]{:S(2)}) collective-permute-start(bf16[1024,512]{1,0:T(8,128)(2,1)} %shard_map.47.refs_0_), channel_id=1, source_target_pairs={{0,32},{16,112},{32,64},{48,16},{64,96},{80,48},{96,0},{112,80},{1... | collective-permute-start | bytes 3145736 | tf_op jit(solution)/shard_map/ppermute | solution.py:215
  10.8 14.6 %collective-permute-start.11 = (bf16[1024,512]{1,0:T(8,128)(2,1)}, bf16[1024,512]{1,0:T(8,128)(2,1)S(1)}, u32[]{:S(2)}, u32[]{:S(2)}) collective-permute-start(bf16[1024,512]{1,0:T(8,128)(2,1)} %shard_map.47.refs_0_), channel_id=1, source_target_pairs={{0,16},{16,0},{32,48},{48,32},{64,80},{80,64},{96,112},{112,96},{1... | collective-permute-start | bytes 3145736 | tf_op jit(solution)/shard_map/ppermute | solution.py:216
  20.0 14.7 %collective-permute-start.3 = (bf16[96,5248]{1,0:T(8,128)(2,1)}, bf16[96,5248]{1,0:T(8,128)(2,1)}, u32[]{:S(2)}, u32[]{:S(2)}) collective-permute-start(bf16[96,5248]{1,0:T(8,128)(2,1)} %collective-permute-done.1.refs_2_), channel_id=1, source_target_pairs={{0,1},{1,2},{2,3},{3,0},{4,5},{5,6},{6,7},{7,4},{8,9},{9,10},{10,1... | collective-permute-start | bytes 3022856 | tf_op jit(solution)/shard_map/ppermute | solution.py:220
  21.6 14.7 %collective-permute-start.2 = (bf16[96,5248]{1,0:T(8,128)(2,1)}, bf16[96,5248]{1,0:T(8,128)(2,1)}, u32[]{:S(2)}, u32[]{:S(2)}) collective-permute-start(bf16[96,5248]{1,0:T(8,128)(2,1)} %collective-permute-done.refs_1_), channel_id=1, source_target_pairs={{0,4},{1,5},{2,6},{3,7},{4,8},{5,9},{6,10},{7,11},{8,12},{9,13},{1... | collective-permute-start | bytes 3022856 | tf_op jit(solution)/shard_map/ppermute | solution.py:219
  25.4 16.0 %collective-permute-start.12 = (bf16[1024,512]{1,0:T(8,128)(2,1)S(1)}, bf16[1024,512]{1,0:T(8,128)(2,1)S(1)}, u32[]{:S(2)}, u32[]{:S(2)}) collective-permute-start(bf16[1024,512]{1,0:T(8,128)(2,1)S(1)} %collective-permute-done.10.refs_1_), channel_id=1, source_target_pairs={{0,32},{16,112},{32,64},{48,16},{64,96},{80,48},{96,0},{112,80},{1... | collective-permute-start | bytes 3145736 | tf_op jit(solution)/shard_map/ppermute | solution.py:215
  25.8 15.6 %collective-permute-start.13 = (bf16[1024,512]{1,0:T(8,128)(2,1)S(1)}, bf16[1024,512]{1,0:T(8,128)(2,1)S(1)}, u32[]{:S(2)}, u32[]{:S(2)}) collective-permute-start(bf16[1024,512]{1,0:T(8,128)(2,1)S(1)} %collective-permute-done.10.refs_1_), channel_id=1, source_target_pairs={{0,16},{16,0},{32,48},{48,32},{64,80},{80,64},{96,112},{112,96},{1... | collective-permute-start | bytes 3145736 | tf_op jit(solution)/shard_map/ppermute | solution.py:216
  25.8 21.2 %collective-permute-start.5 = (bf16[96,5248]{1,0:T(8,128)(2,1)}, bf16[96,5248]{1,0:T(8,128)(2,1)S(1)}, u32[]{:S(2)}, u32[]{:S(2)}) collective-permute-start(bf16[96,5248]{1,0:T(8,128)(2,1)} %collective-permute-done.1.refs_2_), channel_id=1, source_target_pairs={{0,4},{1,5},{2,6},{3,7},{4,8},{5,9},{6,10},{7,11},{8,12},{9,13},{1... | collective-permute-start | bytes 3022856 | tf_op jit(solution)/shard_map/ppermute | solution.py:219
  36.3 14.6 %collective-permute-start.4 = (bf16[96,5248]{1,0:T(8,128)(2,1)}, bf16[96,5248]{1,0:T(8,128)(2,1)S(1)}, u32[]{:S(2)}, u32[]{:S(2)}) collective-permute-start(bf16[96,5248]{1,0:T(8,128)(2,1)} %collective-permute-done.2.refs_3_), channel_id=1, source_target_pairs={{0,1},{1,2},{2,3},{3,0},{4,5},{5,6},{6,7},{7,4},{8,9},{9,10},{10,1... | collective-permute-start | bytes 3022856 | tf_op jit(solution)/shard_map/ppermute | solution.py:220
  41.4 1.0 copy-start.2
  42.4 16.1 %collective-permute-start.14 = (bf16[1024,512]{1,0:T(8,128)(2,1)S(1)}, bf16[1024,512]{1,0:T(8,128)(2,1)}, u32[]{:S(2)}, u32[]{:S(2)}) collective-permute-start(bf16[1024,512]{1,0:T(8,128)(2,1)S(1)} %collective-permute-done.12.refs_2_), channel_id=1, source_target_pairs={{0,32},{16,112},{32,64},{48,16},{64,96},{80,48},{96,0},{112,80},{1... | collective-permute-start | bytes 3145736 | tf_op jit(solution)/shard_map/ppermute | solution.py:215
  42.4 17.7 %collective-permute-start.15 = (bf16[1024,512]{1,0:T(8,128)(2,1)S(1)}, bf16[1024,512]{1,0:T(8,128)(2,1)S(1)}, u32[]{:S(2)}, u32[]{:S(2)}) collective-permute-start(bf16[1024,512]{1,0:T(8,128)(2,1)S(1)} %collective-permute-done.12.refs_2_), channel_id=1, source_target_pairs={{0,16},{16,0},{32,48},{48,32},{64,80},{80,64},{96,112},{112,96},{1... | collective-permute-start | bytes 3145736 | tf_op jit(solution)/shard_map/ppermute | solution.py:216
  47.0 1.0 copy-start.6
  48.0 15.5 %collective-permute-start.7 = (bf16[96,5248]{1,0:T(8,128)(2,1)}, bf16[96,5248]{1,0:T(8,128)(2,1)S(1)}, u32[]{:S(2)}, u32[]{:S(2)}) collective-permute-start(bf16[96,5248]{1,0:T(8,128)(2,1)} %collective-permute-done.3.refs_4_), channel_id=1, source_target_pairs={{0,4},{1,5},{2,6},{3,7},{4,8},{5,9},{6,10},{7,11},{8,12},{9,13},{1... | collective-permute-start | bytes 3022856 | tf_op jit(solution)/shard_map/ppermute | solution.py:219
  50.9 14.5 %collective-permute-start.6 = (bf16[96,5248]{1,0:T(8,128)(2,1)S(1)}, bf16[96,5248]{1,0:T(8,128)(2,1)}, u32[]{:S(2)}, u32[]{:S(2)}) collective-permute-start(bf16[96,5248]{1,0:T(8,128)(2,1)S(1)} %collective-permute-done.4.refs_1_), channel_id=1, source_target_pairs={{0,1},{1,2},{2,3},{3,0},{4,5},{5,6},{6,7},{7,4},{8,9},{9,10},{10,1... | collective-permute-start | bytes 3022856 | tf_op jit(solution)/shard_map/ppermute | solution.py:220
  50.9 1.0 copy-start.8
  51.8 22.5 %collective-permute-start.20 = (bf16[96,5248]{1,0:T(8,128)(2,1)}, bf16[96,5248]{1,0:T(8,128)(2,1)}, u32[]{:S(2)}, u32[]{:S(2)}) collective-permute-start(bf16[96,5248]{1,0:T(8,128)(2,1)} %collective-permute-done.2.refs_3_), channel_id=1, source_target_pairs={{0,4},{1,5},{2,6},{3,7},{4,8},{5,9},{6,10},{7,11},{8,12},{9,13},{1... | collective-permute-start | bytes 3022856 | tf_op jit(solution)/shard_map/ppermute | solution.py:219
  58.5 17.6 %collective-permute-start.17 = (bf16[96,5248]{1,0:T(8,128)(2,1)}, bf16[96,5248]{1,0:T(8,128)(2,1)}, u32[]{:S(2)}, u32[]{:S(2)}) collective-permute-start(bf16[96,5248]{1,0:T(8,128)(2,1)} %collective-permute-done.3.refs_4_), channel_id=1, source_target_pairs={{0,1},{1,2},{2,3},{3,0},{4,5},{5,6},{6,7},{7,4},{8,9},{9,10},{10,1... | collective-permute-start | bytes 3022856 | tf_op jit(solution)/shard_map/ppermute | solution.py:220
  60.1 1.0 copy-start.4
  61.1 18.4 %collective-permute-start.16 = (bf16[1024,512]{1,0:T(8,128)(2,1)}, bf16[1024,512]{1,0:T(8,128)(2,1)}, u32[]{:S(2)}, u32[]{:S(2)}) collective-permute-start(bf16[1024,512]{1,0:T(8,128)(2,1)} %collective-permute-done.14.refs_3_), channel_id=1, source_target_pairs={{0,16},{16,0},{32,48},{48,32},{64,80},{80,64},{96,112},{112,96},{1... | collective-permute-start | bytes 3145736 | tf_op jit(solution)/shard_map/ppermute | solution.py:216
  63.5 1.0 copy-start.10
  65.3 20.3 %collective-permute-start.8 = (bf16[96,5248]{1,0:T(8,128)(2,1)}, bf16[96,5248]{1,0:T(8,128)(2,1)}, u32[]{:S(2)}, u32[]{:S(2)}) collective-permute-start(bf16[96,5248]{1,0:T(8,128)(2,1)} %collective-permute-done.6.refs_1_), channel_id=1, source_target_pairs={{0,4},{1,5},{2,6},{3,7},{4,8},{5,9},{6,10},{7,11},{8,12},{9,13},{1... | collective-permute-start | bytes 3022856 | tf_op jit(solution)/shard_map/ppermute | solution.py:219
  76.1 29.6 %collective-permute-start.21 = (bf16[96,5248]{1,0:T(8,128)(2,1)}, bf16[96,5248]{1,0:T(8,128)(2,1)S(1)}, u32[]{:S(2)}, u32[]{:S(2)}) collective-permute-start(bf16[96,5248]{1,0:T(8,128)(2,1)} %collective-permute-done.20.refs_2_), channel_id=1, source_target_pairs={{0,1},{1,2},{2,3},{3,0},{4,5},{5,6},{6,7},{7,4},{8,9},{9,10},{10,1... | collective-permute-start | bytes 3022856 | tf_op jit(solution)/shard_map/ppermute | solution.py:220
  76.1 29.6 %collective-permute-start.19 = (bf16[96,5248]{1,0:T(8,128)(2,1)}, bf16[96,5248]{1,0:T(8,128)(2,1)S(1)}, u32[]{:S(2)}, u32[]{:S(2)}) collective-permute-start(bf16[96,5248]{1,0:T(8,128)(2,1)} %collective-permute-done.17.refs_3_), channel_id=1, source_target_pairs={{0,4},{1,5},{2,6},{3,7},{4,8},{5,9},{6,10},{7,11},{8,12},{9,13},{1... | collective-permute-start | bytes 3022856 | tf_op jit(solution)/shard_map/ppermute | solution.py:219
  77.7 35.8 %collective-permute-start.18 = (bf16[96,5248]{1,0:T(8,128)(2,1)}, bf16[96,5248]{1,0:T(8,128)(2,1)S(1)}, u32[]{:S(2)}, u32[]{:S(2)}) collective-permute-start(bf16[96,5248]{1,0:T(8,128)(2,1)} %collective-permute-done.6.refs_1_), channel_id=1, source_target_pairs={{0,1},{1,2},{2,3},{3,0},{4,5},{5,6},{6,7},{7,4},{8,9},{9,10},{10,1... | collective-permute-start | bytes 3022856 | tf_op jit(solution)/shard_map/ppermute | solution.py:220
  79.5 1.2 %copy-start = (bf16[1024,512]{1,0:T(8,128)(2,1)S(1)}, bf16[1024,512]{1,0:T(8,128)(2,1)}, u32[]{:S(2)}) copy-start(bf16[1024,512]{1,0:T(8,128)(2,1)} %shard_map.47.refs_0_) | copy-start | bytes 3145732
  80.7 1.2 %copy-start.3 = (bf16[1024,512]{1,0:T(8,128)(2,1)S(1)}, bf16[1024,512]{1,0:T(8,128)(2,1)}, u32[]{:S(2)}) copy-start(bf16[1024,512]{1,0:T(8,128)(2,1)} %copy-done.2) | copy-start | bytes 3145732
  82.0 1.2 %copy-start.5 = (bf16[1024,512]{1,0:T(8,128)(2,1)S(1)}, bf16[1024,512]{1,0:T(8,128)(2,1)}, u32[]{:S(2)}) copy-start(bf16[1024,512]{1,0:T(8,128)(2,1)} %copy-done.4) | copy-start | bytes 3145732
  83.2 6.4 %copy-start.1 = (bf16[96,5248]{1,0:T(8,128)(2,1)S(1)}, bf16[96,5248]{1,0:T(8,128)(2,1)}, u32[]{:S(2)}) copy-start(bf16[96,5248]{1,0:T(8,128)(2,1)} %shard_map.46.refs_0_) | copy-start | bytes 3022852
  85.6 12.9 %copy-start.7 = (bf16[96,5248]{1,0:T(8,128)(2,1)S(1)}, bf16[96,5248]{1,0:T(8,128)(2,1)}, u32[]{:S(2)}) copy-start(bf16[96,5248]{1,0:T(8,128)(2,1)} %copy-done.6) | copy-start | bytes 3022852
  85.6 12.9 %copy-start.9 = (bf16[96,5248]{1,0:T(8,128)(2,1)S(1)}, bf16[96,5248]{1,0:T(8,128)(2,1)}, u32[]{:S(2)}) copy-start(bf16[96,5248]{1,0:T(8,128)(2,1)} %copy-done.8) | copy-start | bytes 3022852
  85.7 32.9 %collective-permute-start.9 = (bf16[96,5248]{1,0:T(8,128)(2,1)}, bf16[96,5248]{1,0:T(8,128)(2,1)S(1)}, u32[]{:S(2)}, u32[]{:S(2)}) collective-permute-start(bf16[96,5248]{1,0:T(8,128)(2,1)} %collective-permute-done.8.refs_0_), channel_id=1, source_target_pairs={{0,1},{1,2},{2,3},{3,0},{4,5},{5,6},{6,7},{7,4},{8,9},{9,10},{10,1... | collective-permute-start | bytes 3022856 | tf_op jit(solution)/shard_map/ppermute | solution.py:220
  98.5 7.2 %copy-start.11 = (bf16[96,5248]{1,0:T(8,128)(2,1)S(1)}, bf16[96,5248]{1,0:T(8,128)(2,1)}, u32[]{:S(2)}) copy-start(bf16[96,5248]{1,0:T(8,128)(2,1)} %copy-done.10) | copy-start | bytes 3022852

commit v3 on v2

--- a/solution.py
+++ b/solution.py
@@ -66,26 +66,22 @@
 def mm_kernel(spots, chunks, offs, *refs):
     n = len(spots)
     amps, ints = refs[:n], refs[n]
-    out, land, wide, done, amp_sems, out_sems = refs[-6:]
+    out, wide, done, out_sems = refs[-4:]
     rows = amps[0].shape[0]
     place = [pl.ds(i * rows, rows) for i in range(n)]
-    loads = [pltpu.make_async_copy(amps[i], land.at[place[i]], amp_sems.at[i]) for i in range(n)]
     stores = [
         pltpu.make_async_copy(done.at[place[i]], out.at[pl.ds(pl.multiple_of(offs[spots[i]], 16), rows)], out_sems.at[i])
         for i in range(n)
     ]
-    for load in loads:
-        load.start()
-
     def fill(i):
         here = slice(i * rows, (i + 1) * rows)
-        code = land[here, SLOTS * TILE :]
+        code = amps[i][:, SLOTS * TILE :]
         zero = jnp.zeros((rows, TILE), BF)
         alpha = jnp.where(code < 0, zero, code)
         beta = jnp.where(code < 0, zero - code, zero + SLOTS)
 
         def slot(j):
-            return land[here, j * TILE : (j + 1) * TILE]
+            return amps[i][:, j * TILE : (j + 1) * TILE]
 
         for t in range(KT):
             if t < FOLD:
@@ -101,7 +97,6 @@
     first = 0
     for size in chunks:
         for i in range(first, first + size):
-            loads[i].wait()
             fill(i)
         here = slice(first * rows, (first + size) * rows)
         done[here, :] = jnp.dot(wide[here, :], ints[...], preferred_element_type=jnp.float32).astype(BF)
@@ -116,7 +111,7 @@
     rows = sum(v.shape[0] for v in amps)
     cols = ints.shape[1]
     anywhere = pl.BlockSpec(memory_space=pl.ANY)
-    in_specs = [pl.BlockSpec(memory_space=pltpu.SMEM)] + [anywhere] * len(amps) + [pl.BlockSpec(memory_space=pltpu.VMEM)]
+    in_specs = [pl.BlockSpec(memory_space=pltpu.SMEM)] + [pl.BlockSpec(memory_space=pltpu.VMEM)] * (len(amps) + 1)
     args = [offs] + list(amps) + [ints]
     alias = {}
     if out is not None:
@@ -129,10 +124,8 @@
         in_specs=in_specs,
         out_specs=anywhere,
         scratch_shapes=[
-            pltpu.VMEM((rows, WIDE), BF),
             pltpu.VMEM((rows, KT * TILE), BF),
             pltpu.VMEM((rows, cols), BF),
-            pltpu.SemaphoreType.DMA((len(amps),)),
             pltpu.SemaphoreType.DMA((len(amps),)),
         ],
         input_output_aliases=alias,
@@ -222,7 +215,7 @@
     x, z = me // 4, me % 4
     spot = jnp.arange(16)
     offs = ((x - sign * (spot // 4) + 4) % 4 * 4 + (z - sign * (spot % 4) + 4) % 4) * dev_rows
-    offs = offs.astype(jnp.int32)
+    offs = jnp.concatenate([offs, offs[15:] + dev_rows // 2]).astype(jnp.int32)
     total = 16 * dev_rows
 
     b10, b01 = by_x(own), by_z(own)
@@ -232,19 +225,20 @@
     i2, s1 = by_y(after(i1, s0, b10, b01)), swap(i1)
     b21, b30, b03, b12 = by_z(after(b20, b02)), by_x(after(b20, b02)), by_z(b02), by_x(after(b02, b11))
     i3, s2 = by_y(after(i2, s1, b20, b02)), swap(i2)
-    s3 = swap(after(i3, s2))
+    s3 = swap(after(i3, s2, b03, b30))
     b22 = by_z(after(b21, b11))
     places = jnp.concatenate([(y - sign * step + 4) % 4 * 2 + core, (y + sign * step + 4) % 4 * 2 + 1 - core])
     ints = join([i0, i1, i2, i3, s0, s1, s2, s3], places)
 
     b13, b31 = by_x(after(b03, b12)), by_z(after(b30, b03))
     b32, b23 = by_x(after(b22, b12)), by_z(after(b22, b03))
-    b33 = by_z(b32)
-    out = multiply([own, b10, b01, b20, b02], [0, 4, 1, 8, 2], [2, 3], offs, ints, None, total)
-    out = multiply([b11, b21, b30, b03], [5, 9, 12, 3], [2, 2], offs, ints, out, total)
-    out = multiply([b12, b22, b13, b31], [6, 10, 7, 13], [2, 2], offs, ints, out, total)
-    out = multiply([b32, b23], [14, 11], [2], offs, ints, out, total)
-    return multiply([b33], [15], [1], offs, ints, out, total)
+    out = multiply([own, b10, b01, b20, b02], [0, 4, 1, 8, 2], [5], offs, ints, None, total)
+    half = dev_rows // 2
+    b32, b23, out = lax.optimization_barrier((b32, b23, out))
+    b33, b33_low = by_z(b32[:half]), by_x(b23[half:])
+    out = multiply([b11, b21, b30, b03, b12, b22], [5, 9, 12, 3, 6, 10], [6], offs, ints, out, total)
+    out = multiply([b13, b31, b32, b23], [7, 13, 14, 11], [4], offs, ints, out, total)
+    return multiply([b33, b33_low], [15, 16], [2], offs, ints, out, total)
 
 
 def solution(mesh):

time: 124 us -> 117 us (0.944); the launches traced: 122 us -> 117 us
  local copies, waits for them, and re-layouts: 8.52 us -> 17.9 us
  Pallas kernels: 40.2 us -> 31.3 us
  waiting for transfers between devices: 49.7 us -> 43.6 us
    pallas_call x5 -> x4, Pallas kernels: 32 us -> 22.8 us  [multiply(): pl.pallas_call(functools.partial(mm_kernel, tuple(spots), tuple(chunks)),...]
    unnamed x24 -> x48, local copies, waits for them, and re-layouts: 8.52 us -> 17.2 us
    ppermute x3, waiting for transfers between devices: 12.6 us -> 5.48 us  [on_device(): lax.ppermute(v, 'row', [(r, (r + (2 if r % 2 == 0 else -2)) % 8) for r in...]
    ppermute x8, waiting for transfers between devices: 19.1 us -> 22.3 us  [on_device(): by_z = lambda v: lax.ppermute(v, ('row', 'col'), along_z)]
    ppermute x8, starting transfers between devices: 10.9 us -> 7.93 us  [on_device(): by_z = lambda v: lax.ppermute(v, ('row', 'col'), along_z)]
    ppermute x7 -> x8, starting transfers between devices: 10.1 us -> 13 us  [on_device(): by_x = lambda v: lax.ppermute(v, ('row', 'col'), along_x)]
    ppermute x7 -> x8, waiting for transfers between devices: 18 us -> 15.9 us  [on_device(): by_x = lambda v: lax.ppermute(v, ('row', 'col'), along_x)]
  transfers between devices with their start and end apart: 22 -> 23, of which waited for: 13 -> 12; matrix products, arithmetic and copies ran while one was open for 0% -> 1% of each run, Pallas kernels for 28% -> 21%
where the time goes in v3:
time: 117 us
  waiting for transfers between devices  43.6 us (37%)
  Pallas kernels  31.3 us (27%)
  starting transfers between devices  22.9 us (20%)
  local copies, waits for them, and re-layouts  17.9 us (15%)
    pallas_call x4, Pallas kernels, multiply(): pl.pallas_call(functools.partial(mm_kernel, tuple(spots), tuple(chunks)),...  22.8 us
    ppermute x8, waiting for transfers between devices, on_device(): by_z = lambda v: lax.ppermute(v, ('row', 'col'), along_z)  22.3 us
    unnamed x48, local copies, waits for them, and re-layouts  17.2 us
    ppermute x8, waiting for transfers between devices, on_device(): by_x = lambda v: lax.ppermute(v, ('row', 'col'), along_x)  15.9 us
    ppermute x8, starting transfers between devices, on_device(): by_x = lambda v: lax.ppermute(v, ('row', 'col'), along_x)  13 us
    ppermute x8, starting transfers between devices, on_device(): by_z = lambda v: lax.ppermute(v, ('row', 'col'), along_z)  7.93 us
    ppermute x3, waiting for transfers between devices, on_device(): lax.ppermute(v, 'row', [(r, (r + (2 if r % 2 == 0 else -2)) % 8) for r in...  5.48 us
    pallas_call x1, Pallas kernels, pack(): pl.pallas_call(pack_kernel, out_shape=[jax.ShapeDtypeStruct((n, WIDE), BF...  3.39 us
  transfers between devices with their start and end apart: 23, of which 12 were waited for; matrix products, arithmetic and copies ran while one was open for 1% of the time, Pallas kernels for 21%

profile of v3, /device:TPU:34, one launch (start us, length us, event | category | flops | bytes accessed | tf_op | source)
XLA Modules:
  0.0 117.0 jit_solution(16440539976405702372)
XLA Ops:
  0.0 3.4 %shard_map.46.refs_0_ = bf16[96,5248]{1,0:T(8,128)(2,1)} custom-call(s32[64,96]{1,0:T(8,128)} %bitcast.2, bf16[96,8192]{1,0:T(8,128)(2,1)} %amps_ref.1), custom_call_target="tpu_custom_call" | custom-call | tf_op jit(solution)/shard_map/pallas_call | solution.py:144
  3.4 1.9 %collective-permute-start.1 = (bf16[96,5248]{1,0:T(8,128)(2,1)}, bf16[96,5248]{1,0:T(8,128)(2,1)S(1)}, u32[]{:S(2)}, u32[]{:S(2)}) collective-permute-start(bf16[96,5248]{1,0:T(8,128)(2,1)} %shard_map.46.refs_0_), channel_id=1, source_target_pairs={{0,1},{1,2},{2,3},{3,0},{4,5},{5,6},{6,7},{7,4},{8,9},{9,10},{10,1... | collective-permute-start | bytes 3022856 | tf_op jit(solution)/shard_map/ppermute | solution.py:213
  5.3 1.5 %collective-permute-start = (bf16[96,5248]{1,0:T(8,128)(2,1)}, bf16[96,5248]{1,0:T(8,128)(2,1)S(1)}, u32[]{:S(2)}, u32[]{:S(2)}) collective-permute-start(bf16[96,5248]{1,0:T(8,128)(2,1)} %shard_map.46.refs_0_), channel_id=1, source_target_pairs={{0,4},{1,5},{2,6},{3,7},{4,8},{5,9},{6,10},{7,11},{8,12},{9,13},{1... | collective-permute-start | bytes 3022856 | tf_op jit(solution)/shard_map/ppermute | solution.py:212
  6.8 2.4 %shard_map.47.refs_0_ = bf16[1024,512]{1,0:T(8,128)(2,1)} custom-call(s32[4,8]{1,0:T(4,128)} %bitcast.3, bf16[1024,512]{1,0:T(8,128)(2,1)} %ints_ref.1), custom_call_target="tpu_custom_call" | custom-call | tf_op jit(solution)/shard_map/pallas_call | solution.py:151
  9.2 1.6 %collective-permute-start.11 = (bf16[1024,512]{1,0:T(8,128)(2,1)}, bf16[1024,512]{1,0:T(8,128)(2,1)S(1)}, u32[]{:S(2)}, u32[]{:S(2)}) collective-permute-start(bf16[1024,512]{1,0:T(8,128)(2,1)} %shard_map.47.refs_0_), channel_id=1, source_target_pairs={{0,32},{16,112},{32,64},{48,16},{64,96},{80,48},{96,0},{112,80},{1... | collective-permute-start | bytes 3145736 | tf_op jit(solution)/shard_map/ppermute | solution.py:208
  10.8 7.2 %collective-permute-done.1.refs_2_ = bf16[96,5248]{1,0:T(8,128)(2,1)S(1)} collective-permute-done((bf16[96,5248]{1,0:T(8,128)(2,1)}, bf16[96,5248]{1,0:T(8,128)(2,1)S(1)}, u32[]{:S(2)}, u32[]{:S(2)}) %collective-permute-start.1) | collective-permute-done | bytes 1007648 | tf_op jit(solution)/shard_map/ppermute | solution.py:213
  18.0 1.9 %collective-permute-done.refs_1_ = bf16[96,5248]{1,0:T(8,128)(2,1)S(1)} collective-permute-done((bf16[96,5248]{1,0:T(8,128)(2,1)}, bf16[96,5248]{1,0:T(8,128)(2,1)S(1)}, u32[]{:S(2)}, u32[]{:S(2)}) %collective-permute-start) | collective-permute-done | bytes 1007648 | tf_op jit(solution)/shard_map/ppermute | solution.py:212
  19.9 1.6 %collective-permute-start.3 = (bf16[96,5248]{1,0:T(8,128)(2,1)S(1)}, bf16[96,5248]{1,0:T(8,128)(2,1)S(1)}, u32[]{:S(2)}, u32[]{:S(2)}) collective-permute-start(bf16[96,5248]{1,0:T(8,128)(2,1)S(1)} %collective-permute-done.1.refs_2_), channel_id=1, source_target_pairs={{0,1},{1,2},{2,3},{3,0},{4,5},{5,6},{6,7},{7,4},{8,9},{9,10},{10,1... | collective-permute-start | bytes 3022856 | tf_op jit(solution)/shard_map/ppermute | solution.py:213
  21.5 1.5 %collective-permute-start.2 = (bf16[96,5248]{1,0:T(8,128)(2,1)S(1)}, bf16[96,5248]{1,0:T(8,128)(2,1)S(1)}, u32[]{:S(2)}, u32[]{:S(2)}) collective-permute-start(bf16[96,5248]{1,0:T(8,128)(2,1)S(1)} %collective-permute-done.refs_1_), channel_id=1, source_target_pairs={{0,4},{1,5},{2,6},{3,7},{4,8},{5,9},{6,10},{7,11},{8,12},{9,13},{1... | collective-permute-start | bytes 3022856 | tf_op jit(solution)/shard_map/ppermute | solution.py:212
  23.0 1.1 copy-done.12
  24.1 1.4 %collective-permute-done.11.refs_1_ = bf16[1024,512]{1,0:T(8,128)(2,1)S(1)} collective-permute-done((bf16[1024,512]{1,0:T(8,128)(2,1)}, bf16[1024,512]{1,0:T(8,128)(2,1)S(1)}, u32[]{:S(2)}, u32[]{:S(2)}) %collective-permute-start.11) | collective-permute-done | bytes 1048608 | tf_op jit(solution)/shard_map/ppermute | solution.py:208
  25.4 1.0 copy-done.2
  26.8 1.2 %collective-permute-start.5 = (bf16[96,5248]{1,0:T(8,128)(2,1)S(1)}, bf16[96,5248]{1,0:T(8,128)(2,1)S(1)}, u32[]{:S(2)}, u32[]{:S(2)}) collective-permute-start(bf16[96,5248]{1,0:T(8,128)(2,1)S(1)} %collective-permute-done.1.refs_2_), channel_id=1, source_target_pairs={{0,4},{1,5},{2,6},{3,7},{4,8},{5,9},{6,10},{7,11},{8,12},{9,13},{1... | collective-permute-start | bytes 3022856 | tf_op jit(solution)/shard_map/ppermute | solution.py:212
  28.0 1.0 copy-done.10
  29.0 5.3 %collective-permute-done.3.refs_4_ = bf16[96,5248]{1,0:T(8,128)(2,1)S(1)} collective-permute-done((bf16[96,5248]{1,0:T(8,128)(2,1)S(1)}, bf16[96,5248]{1,0:T(8,128)(2,1)S(1)}, u32[]{:S(2)}, u32[]{:S(2)}) %collective-permute-start.3) | collective-permute-done | bytes 1007648 | tf_op jit(solution)/shard_map/ppermute | solution.py:213
  34.2 1.6 %collective-permute-done.2.refs_3_ = bf16[96,5248]{1,0:T(8,128)(2,1)S(1)} collective-permute-done((bf16[96,5248]{1,0:T(8,128)(2,1)S(1)}, bf16[96,5248]{1,0:T(8,128)(2,1)S(1)}, u32[]{:S(2)}, u32[]{:S(2)}) %collective-permute-start.2) | collective-permute-done | bytes 1007648 | tf_op jit(solution)/shard_map/ppermute | solution.py:212
  35.9 1.5 %collective-permute-start.17 = (bf16[96,5248]{1,0:T(8,128)(2,1)S(1)}, bf16[96,5248]{1,0:T(8,128)(2,1)}, u32[]{:S(2)}, u32[]{:S(2)}) collective-permute-start(bf16[96,5248]{1,0:T(8,128)(2,1)S(1)} %collective-permute-done.2.refs_3_), channel_id=1, source_target_pairs={{0,4},{1,5},{2,6},{3,7},{4,8},{5,9},{6,10},{7,11},{8,12},{9,13},{1... | collective-permute-start | bytes 3022856 | tf_op jit(solution)/shard_map/ppermute | solution.py:212
  37.4 0.9 copy-done.16
  38.3 4.1 %collective-permute-done.13.refs_2_ = bf16[1024,512]{1,0:T(8,128)(2,1)S(1)} collective-permute-done((bf16[1024,512]{1,0:T(8,128)(2,1)S(1)}, bf16[1024,512]{1,0:T(8,128)(2,1)S(1)}, u32[]{:S(2)}, u32[]{:S(2)}) %collective-permute-start.13) | collective-permute-done | bytes 1048608 | tf_op jit(solution)/shard_map/ppermute | solution.py:208
  42.4 1.0 copy-done.6
  43.4 1.0 copy-done.4
  44.4 2.3 %collective-permute-done.5.refs_0_ = bf16[96,5248]{1,0:T(8,128)(2,1)S(1)} collective-permute-done((bf16[96,5248]{1,0:T(8,128)(2,1)S(1)}, bf16[96,5248]{1,0:T(8,128)(2,1)S(1)}, u32[]{:S(2)}, u32[]{:S(2)}) %collective-permute-start.5) | collective-permute-done | bytes 1007648 | tf_op jit(solution)/shard_map/ppermute | solution.py:212
  46.7 1.0 copy-done.18
  47.6 2.6 %collective-permute-done.4.refs_1_ = bf16[96,5248]{1,0:T(8,128)(2,1)S(1)} collective-permute-done((bf16[96,5248]{1,0:T(8,128)(2,1)S(1)}, bf16[96,5248]{1,0:T(8,128)(2,1)S(1)}, u32[]{:S(2)}, u32[]{:S(2)}) %collective-permute-start.4) | collective-permute-done | bytes 1007648 | tf_op jit(solution)/shard_map/ppermute | solution.py:213
  50.2 1.5 %collective-permute-start.7 = (bf16[96,5248]{1,0:T(8,128)(2,1)S(1)}, bf16[96,5248]{1,0:T(8,128)(2,1)S(1)}, u32[]{:S(2)}, u32[]{:S(2)}) collective-permute-start(bf16[96,5248]{1,0:T(8,128)(2,1)S(1)} %collective-permute-done.3.refs_4_), channel_id=1, source_target_pairs={{0,4},{1,5},{2,6},{3,7},{4,8},{5,9},{6,10},{7,11},{8,12},{9,13},{1... | collective-permute-start | bytes 3022856 | tf_op jit(solution)/shard_map/ppermute | solution.py:212
  51.7 1.0 copy-done.14
  52.7 4.9 %collective-permute-done.17.refs_2_ = bf16[96,5248]{1,0:T(8,128)(2,1)} collective-permute-done((bf16[96,5248]{1,0:T(8,128)(2,1)S(1)}, bf16[96,5248]{1,0:T(8,128)(2,1)}, u32[]{:S(2)}, u32[]{:S(2)}) %collective-permute-start.17) | collective-permute-done | bytes 1007648 | tf_op jit(solution)/shard_map/ppermute | solution.py:212
  57.6 1.0 copy-done.20
  58.6 3.5 %collective-permute-done.9.refs_3_ = bf16[96,5248]{1,0:T(8,128)(2,1)} collective-permute-done((bf16[96,5248]{1,0:T(8,128)(2,1)S(1)}, bf16[96,5248]{1,0:T(8,128)(2,1)}, u32[]{:S(2)}, u32[]{:S(2)}) %collective-permute-start.9) | collective-permute-done | bytes 1007648 | tf_op jit(solution)/shard_map/ppermute | solution.py:213
  62.1 1.0 copy-done.8
  63.1 5.2 %collective-permute-done.7.refs_4_ = bf16[96,5248]{1,0:T(8,128)(2,1)S(1)} collective-permute-done((bf16[96,5248]{1,0:T(8,128)(2,1)S(1)}, bf16[96,5248]{1,0:T(8,128)(2,1)S(1)}, u32[]{:S(2)}, u32[]{:S(2)}) %collective-permute-start.7) | collective-permute-done | bytes 1007648 | tf_op jit(solution)/shard_map/ppermute | solution.py:212
  68.3 1.0 copy-done.22
  69.2 3.7 %collective-permute-done.6.refs_5_ = bf16[96,5248]{1,0:T(8,128)(2,1)} collective-permute-done((bf16[96,5248]{1,0:T(8,128)(2,1)S(1)}, bf16[96,5248]{1,0:T(8,128)(2,1)}, u32[]{:S(2)}, u32[]{:S(2)}) %collective-permute-start.6) | collective-permute-done | bytes 1007648 | tf_op jit(solution)/shard_map/ppermute | solution.py:213
  72.9 1.5 %collective-permute-start.8 = (bf16[96,5248]{1,0:T(8,128)(2,1)}, bf16[96,5248]{1,0:T(8,128)(2,1)S(1)}, u32[]{:S(2)}, u32[]{:S(2)}) collective-permute-start(bf16[96,5248]{1,0:T(8,128)(2,1)} %collective-permute-done.6.refs_5_), channel_id=1, source_target_pairs={{0,4},{1,5},{2,6},{3,7},{4,8},{5,9},{6,10},{7,11},{8,12},{9,13},{1... | collective-permute-start | bytes 3022856 | tf_op jit(solution)/shard_map/ppermute | solution.py:212
  75.7 1.3 %collective-permute-start.22 = (bf16[96,5248]{1,0:T(8,128)(2,1)}, bf16[96,5248]{1,0:T(8,128)(2,1)S(1)}, u32[]{:S(2)}, u32[]{:S(2)}) collective-permute-start(bf16[96,5248]{1,0:T(8,128)(2,1)} %collective-permute-done.17.refs_2_), channel_id=1, source_target_pairs={{0,1},{1,2},{2,3},{3,0},{4,5},{5,6},{6,7},{7,4},{8,9},{9,10},{10,1... | collective-permute-start | bytes 3022856 | tf_op jit(solution)/shard_map/ppermute | solution.py:213
  77.0 1.2 %collective-permute-start.21 = (bf16[96,5248]{1,0:T(8,128)(2,1)}, bf16[96,5248]{1,0:T(8,128)(2,1)S(1)}, u32[]{:S(2)}, u32[]{:S(2)}) collective-permute-start(bf16[96,5248]{1,0:T(8,128)(2,1)} %collective-permute-done.9.refs_3_), channel_id=1, source_target_pairs={{0,4},{1,5},{2,6},{3,7},{4,8},{5,9},{6,10},{7,11},{8,12},{9,13},{1... | collective-permute-start | bytes 3022856 | tf_op jit(solution)/shard_map/ppermute | solution.py:212
  78.3 1.2 %copy-done = bf16[1024,512]{1,0:T(8,128)(2,1)S(1)} copy-done((bf16[1024,512]{1,0:T(8,128)(2,1)S(1)}, bf16[1024,512]{1,0:T(8,128)(2,1)}, u32[]{:S(2)}) %copy-start) | copy-done | bytes 1048600
  79.6 1.2 %copy-done.3 = bf16[1024,512]{1,0:T(8,128)(2,1)S(1)} copy-done((bf16[1024,512]{1,0:T(8,128)(2,1)S(1)}, bf16[1024,512]{1,0:T(8,128)(2,1)}, u32[]{:S(2)}) %copy-start.3) | copy-done | bytes 1048600
  80.8 1.2 %copy-done.5 = bf16[1024,512]{1,0:T(8,128)(2,1)S(1)} copy-done((bf16[1024,512]{1,0:T(8,128)(2,1)S(1)}, bf16[1024,512]{1,0:T(8,128)(2,1)}, u32[]{:S(2)}) %copy-start.5) | copy-done | bytes 1048600
  82.0 1.2 %copy-done.7 = bf16[1024,512]{1,0:T(8,128)(2,1)S(1)} copy-done((bf16[1024,512]{1,0:T(8,128)(2,1)S(1)}, bf16[1024,512]{1,0:T(8,128)(2,1)}, u32[]{:S(2)}) %copy-start.7) | copy-done | bytes 1048600
  83.2 1.2 %copy-done.9 = bf16[1024,512]{1,0:T(8,128)(2,1)S(1)} copy-done((bf16[1024,512]{1,0:T(8,128)(2,1)S(1)}, bf16[1024,512]{1,0:T(8,128)(2,1)}, u32[]{:S(2)}) %copy-start.9) | copy-done | bytes 1048600
  84.5 2.8 %shard_map.48.refs_5_.refs_6_.refs_4_.refs_2_ = bf16[8192,512]{1,0:T(8,128)(2,1)S(1)} custom-call(s32[8]{0:T(128)S(1)} %pad_add_fusion.1.offs, bf16[1024,512]{1,0:T(8,128)(2,1)S(1)} %copy-done, bf16[1024,512]{1,0:T(8,128)(2,1)S(1)} %collective-permute-done.11.refs_1_, bf16[1024,512]{1,0:T(8,128)(2,1)S(1)} %copy-done.5, ...), custom_call_target="tpu_custom_call" | custom-call | tf_op jit(solution)/shard_map/pallas_call | solution.py:187
  87.5 6.4 %shard_map.49.refs_7_ = bf16[1536,512]{1,0:T(8,128)(2,1)} custom-call(s32[17]{0:T(128)S(1)} %pad_add_fusion.offs, bf16[96,5248]{1,0:T(8,128)(2,1)S(1)} %copy-done.1, bf16[96,5248]{1,0:T(8,128)(2,1)S(1)} %copy-done.13, bf16[96,5248]{1,0:T(8,128)(2,1)S(1)} %copy-done.11, bf16[96,5248]{1,0:T(8,128)(2,1)S(1)} %copy-done.17, bf16[96,5248]{1,0:T(8,128)(2,1)S(1)} %copy-done.15, ...), custom_call_target="tpu_custom_call" | custom-call | flops 4026531840 | bytes 13918208 | tf_op jit(solution)/shard_map/pallas_call | solution.py:121
  94.0 3.1 %collective-permute-start.19 = (bf16[48,5248]{1,0:T(8,128)(2,1)S(1)}, bf16[48,5248]{1,0:T(8,128)(2,1)S(1)}, u32[]{:S(2)}, u32[]{:S(2)}) collective-permute-start(bf16[48,5248]{1,0:T(8,128)(2,1)S(1)} %slice.10), channel_id=1, source_target_pairs={{0,1},{1,2},{2,3},{3,0},{4,5},{5,6},{6,7},{7,4},{8,9},{9,10},{10,1... | collective-permute-start | bytes 1511432 | tf_op jit(solution)/shard_map/ppermute | solution.py:213
  97.1 3.2 %collective-permute-start.20 = (bf16[48,5248]{1,0:T(8,128)(2,1)S(1)}, bf16[48,5248]{1,0:T(8,128)(2,1)S(1)}, u32[]{:S(2)}, u32[]{:S(2)}) collective-permute-start(bf16[48,5248]{1,0:T(8,128)(2,1)S(1)} %slice.11), channel_id=1, source_target_pairs={{0,4},{1,5},{2,6},{3,7},{4,8},{5,9},{6,10},{7,11},{8,12},{9,13},{1... | collective-permute-start | bytes 1511432 | tf_op jit(solution)/shard_map/ppermute | solution.py:212
  100.3 8.3 %shard_map.50.refs_5_ = bf16[1536,512]{1,0:T(8,128)(2,1)} custom-call(s32[17]{0:T(128)S(1)} %pad_add_fusion.offs, bf16[96,5248]{1,0:T(8,128)(2,1)S(1)} %copy-done.19, bf16[96,5248]{1,0:T(8,128)(2,1)S(1)} %copy-done.21, bf16[96,5248]{1,0:T(8,128)(2,1)} %collective-permute-done.17.refs_2_, ...), custom_call_target="tpu_custom_call", output_to_operand_aliasing={{}: (8, {})} | custom-call | flops 4831838208 | bytes 15024128 | tf_op jit(solution)/shard_map/pallas_call | solution.py:121
  108.6 5.3 %shard_map.51.refs_3_ = bf16[1536,512]{1,0:T(8,128)(2,1)} custom-call(s32[17]{0:T(128)S(1)} %pad_add_fusion.offs, bf16[96,5248]{1,0:T(8,128)(2,1)S(1)} %collective-permute-done.21.refs_0_, bf16[96,5248]{1,0:T(8,128)(2,1)S(1)} %collective-permute-done.22.refs_1_, bf16[96,5248]{1,0:T(8,128)(2,1)S(1)} %collective-permute-done.8.refs_2_, ...), custom_call_target="tpu_custom_call", output_to_operand_aliasing={{}: (6, {})} | custom-call | flops 3221225472 | bytes 12812288 | tf_op jit(solution)/shard_map/pallas_call | solution.py:121
  114.0 2.8 %shard_map.52 = bf16[1536,512]{1,0:T(8,128)(2,1)} custom-call(s32[17]{0:T(128)S(1)} %pad_add_fusion.offs, bf16[48,5248]{1,0:T(8,128)(2,1)S(1)} %collective-permute-done.19.refs_0_, bf16[48,5248]{1,0:T(8,128)(2,1)S(1)} %collective-permute-done.20.refs_1_, ...), custom_call_target="tpu_custom_call", output_to_operand_aliasing={{}: (4, {})} | custom-call | flops 805306368 | bytes 9494528 | tf_op jit(solution)/shard_map/pallas_call | solution.py:121
  (60 shorter events, 1.6 us)
Async XLA Ops:
  3.4 14.6 %collective-permute-start.1 = (bf16[96,5248]{1,0:T(8,128)(2,1)}, bf16[96,5248]{1,0:T(8,128)(2,1)S(1)}, u32[]{:S(2)}, u32[]{:S(2)}) collective-permute-start(bf16[96,5248]{1,0:T(8,128)(2,1)} %shard_map.46.refs_0_), channel_id=1, source_target_pairs={{0,1},{1,2},{2,3},{3,0},{4,5},{5,6},{6,7},{7,4},{8,9},{9,10},{10,1... | collective-permute-start | bytes 3022856 | tf_op jit(solution)/shard_map/ppermute | solution.py:213
  5.3 14.6 %collective-permute-start = (bf16[96,5248]{1,0:T(8,128)(2,1)}, bf16[96,5248]{1,0:T(8,128)(2,1)S(1)}, u32[]{:S(2)}, u32[]{:S(2)}) collective-permute-start(bf16[96,5248]{1,0:T(8,128)(2,1)} %shard_map.46.refs_0_), channel_id=1, source_target_pairs={{0,4},{1,5},{2,6},{3,7},{4,8},{5,9},{6,10},{7,11},{8,12},{9,13},{1... | collective-permute-start | bytes 3022856 | tf_op jit(solution)/shard_map/ppermute | solution.py:212
  9.2 16.2 %collective-permute-start.11 = (bf16[1024,512]{1,0:T(8,128)(2,1)}, bf16[1024,512]{1,0:T(8,128)(2,1)S(1)}, u32[]{:S(2)}, u32[]{:S(2)}) collective-permute-start(bf16[1024,512]{1,0:T(8,128)(2,1)} %shard_map.47.refs_0_), channel_id=1, source_target_pairs={{0,32},{16,112},{32,64},{48,16},{64,96},{80,48},{96,0},{112,80},{1... | collective-permute-start | bytes 3145736 | tf_op jit(solution)/shard_map/ppermute | solution.py:208
  10.8 14.6 %collective-permute-start.12 = (bf16[1024,512]{1,0:T(8,128)(2,1)}, bf16[1024,512]{1,0:T(8,128)(2,1)S(1)}, u32[]{:S(2)}, u32[]{:S(2)}) collective-permute-start(bf16[1024,512]{1,0:T(8,128)(2,1)} %shard_map.47.refs_0_), channel_id=1, source_target_pairs={{0,16},{16,0},{32,48},{48,32},{64,80},{80,64},{96,112},{112,96},{1... | collective-permute-start | bytes 3145736 | tf_op jit(solution)/shard_map/ppermute | solution.py:209
  19.9 14.4 %collective-permute-start.3 = (bf16[96,5248]{1,0:T(8,128)(2,1)S(1)}, bf16[96,5248]{1,0:T(8,128)(2,1)S(1)}, u32[]{:S(2)}, u32[]{:S(2)}) collective-permute-start(bf16[96,5248]{1,0:T(8,128)(2,1)S(1)} %collective-permute-done.1.refs_2_), channel_id=1, source_target_pairs={{0,1},{1,2},{2,3},{3,0},{4,5},{5,6},{6,7},{7,4},{8,9},{9,10},{10,1... | collective-permute-start | bytes 3022856 | tf_op jit(solution)/shard_map/ppermute | solution.py:213
  21.5 14.4 %collective-permute-start.2 = (bf16[96,5248]{1,0:T(8,128)(2,1)S(1)}, bf16[96,5248]{1,0:T(8,128)(2,1)S(1)}, u32[]{:S(2)}, u32[]{:S(2)}) collective-permute-start(bf16[96,5248]{1,0:T(8,128)(2,1)S(1)} %collective-permute-done.refs_1_), channel_id=1, source_target_pairs={{0,4},{1,5},{2,6},{3,7},{4,8},{5,9},{6,10},{7,11},{8,12},{9,13},{1... | collective-permute-start | bytes 3022856 | tf_op jit(solution)/shard_map/ppermute | solution.py:212
  23.0 1.1 copy-start.12
  25.4 1.0 copy-start.2
  26.4 16.0 %collective-permute-start.13 = (bf16[1024,512]{1,0:T(8,128)(2,1)S(1)}, bf16[1024,512]{1,0:T(8,128)(2,1)S(1)}, u32[]{:S(2)}, u32[]{:S(2)}) collective-permute-start(bf16[1024,512]{1,0:T(8,128)(2,1)S(1)} %collective-permute-done.11.refs_1_), channel_id=1, source_target_pairs={{0,32},{16,112},{32,64},{48,16},{64,96},{80,48},{96,0},{112,80},{1... | collective-permute-start | bytes 3145736 | tf_op jit(solution)/shard_map/ppermute | solution.py:208
  26.8 15.6 %collective-permute-start.14 = (bf16[1024,512]{1,0:T(8,128)(2,1)S(1)}, bf16[1024,512]{1,0:T(8,128)(2,1)S(1)}, u32[]{:S(2)}, u32[]{:S(2)}) collective-permute-start(bf16[1024,512]{1,0:T(8,128)(2,1)S(1)} %collective-permute-done.11.refs_1_), channel_id=1, source_target_pairs={{0,16},{16,0},{32,48},{48,32},{64,80},{80,64},{96,112},{112,96},{1... | collective-permute-start | bytes 3145736 | tf_op jit(solution)/shard_map/ppermute | solution.py:209
  26.8 19.9 %collective-permute-start.5 = (bf16[96,5248]{1,0:T(8,128)(2,1)S(1)}, bf16[96,5248]{1,0:T(8,128)(2,1)S(1)}, u32[]{:S(2)}, u32[]{:S(2)}) collective-permute-start(bf16[96,5248]{1,0:T(8,128)(2,1)S(1)} %collective-permute-done.1.refs_2_), channel_id=1, source_target_pairs={{0,4},{1,5},{2,6},{3,7},{4,8},{5,9},{6,10},{7,11},{8,12},{9,13},{1... | collective-permute-start | bytes 3022856 | tf_op jit(solution)/shard_map/ppermute | solution.py:212
  28.0 1.0 copy-start.10
  35.9 14.4 %collective-permute-start.4 = (bf16[96,5248]{1,0:T(8,128)(2,1)S(1)}, bf16[96,5248]{1,0:T(8,128)(2,1)S(1)}, u32[]{:S(2)}, u32[]{:S(2)}) collective-permute-start(bf16[96,5248]{1,0:T(8,128)(2,1)S(1)} %collective-permute-done.2.refs_3_), channel_id=1, source_target_pairs={{0,1},{1,2},{2,3},{3,0},{4,5},{5,6},{6,7},{7,4},{8,9},{9,10},{10,1... | collective-permute-start | bytes 3022856 | tf_op jit(solution)/shard_map/ppermute | solution.py:213
  35.9 21.7 %collective-permute-start.17 = (bf16[96,5248]{1,0:T(8,128)(2,1)S(1)}, bf16[96,5248]{1,0:T(8,128)(2,1)}, u32[]{:S(2)}, u32[]{:S(2)}) collective-permute-start(bf16[96,5248]{1,0:T(8,128)(2,1)S(1)} %collective-permute-done.2.refs_3_), channel_id=1, source_target_pairs={{0,4},{1,5},{2,6},{3,7},{4,8},{5,9},{6,10},{7,11},{8,12},{9,13},{1... | collective-permute-start | bytes 3022856 | tf_op jit(solution)/shard_map/ppermute | solution.py:212
  37.4 0.9 copy-start.16
  42.4 1.0 copy-start.6
  43.4 18.7 %collective-permute-start.15 = (bf16[1024,512]{1,0:T(8,128)(2,1)S(1)}, bf16[1024,512]{1,0:T(8,128)(2,1)}, u32[]{:S(2)}, u32[]{:S(2)}) collective-permute-start(bf16[1024,512]{1,0:T(8,128)(2,1)S(1)} %collective-permute-done.13.refs_2_), channel_id=1, source_target_pairs={{0,32},{16,112},{32,64},{48,16},{64,96},{80,48},{96,0},{112,80},{1... | collective-permute-start | bytes 3145736 | tf_op jit(solution)/shard_map/ppermute | solution.py:208
  43.4 18.7 %collective-permute-start.16 = (bf16[1024,512]{1,0:T(8,128)(2,1)S(1)}, bf16[1024,512]{1,0:T(8,128)(2,1)S(1)}, u32[]{:S(2)}, u32[]{:S(2)}) collective-permute-start(bf16[1024,512]{1,0:T(8,128)(2,1)S(1)} %collective-permute-done.13.refs_2_), channel_id=1, source_target_pairs={{0,16},{16,0},{32,48},{48,32},{64,80},{80,64},{96,112},{112,96},{1... | collective-permute-start | bytes 3145736 | tf_op jit(solution)/shard_map/ppermute | solution.py:209
  43.4 1.0 copy-start.4
  46.7 1.0 copy-start.18
  47.6 14.5 %collective-permute-start.9 = (bf16[96,5248]{1,0:T(8,128)(2,1)S(1)}, bf16[96,5248]{1,0:T(8,128)(2,1)}, u32[]{:S(2)}, u32[]{:S(2)}) collective-permute-start(bf16[96,5248]{1,0:T(8,128)(2,1)S(1)} %collective-permute-done.3.refs_4_), channel_id=1, source_target_pairs={{0,1},{1,2},{2,3},{3,0},{4,5},{5,6},{6,7},{7,4},{8,9},{9,10},{10,1... | collective-permute-start | bytes 3022856 | tf_op jit(solution)/shard_map/ppermute | solution.py:213
  50.2 18.0 %collective-permute-start.7 = (bf16[96,5248]{1,0:T(8,128)(2,1)S(1)}, bf16[96,5248]{1,0:T(8,128)(2,1)S(1)}, u32[]{:S(2)}, u32[]{:S(2)}) collective-permute-start(bf16[96,5248]{1,0:T(8,128)(2,1)S(1)} %collective-permute-done.3.refs_4_), channel_id=1, source_target_pairs={{0,4},{1,5},{2,6},{3,7},{4,8},{5,9},{6,10},{7,11},{8,12},{9,13},{1... | collective-permute-start | bytes 3022856 | tf_op jit(solution)/shard_map/ppermute | solution.py:212
  51.7 1.0 copy-start.14
  57.6 15.3 %collective-permute-start.6 = (bf16[96,5248]{1,0:T(8,128)(2,1)S(1)}, bf16[96,5248]{1,0:T(8,128)(2,1)}, u32[]{:S(2)}, u32[]{:S(2)}) collective-permute-start(bf16[96,5248]{1,0:T(8,128)(2,1)S(1)} %collective-permute-done.4.refs_1_), channel_id=1, source_target_pairs={{0,1},{1,2},{2,3},{3,0},{4,5},{5,6},{6,7},{7,4},{8,9},{9,10},{10,1... | collective-permute-start | bytes 3022856 | tf_op jit(solution)/shard_map/ppermute | solution.py:213
  57.6 1.0 copy-start.20
  62.1 1.0 copy-start.8
  63.1 15.3 %collective-permute-start.18 = (bf16[1024,512]{1,0:T(8,128)(2,1)}, bf16[1024,512]{1,0:T(8,128)(2,1)}, u32[]{:S(2)}, u32[]{:S(2)}) collective-permute-start(bf16[1024,512]{1,0:T(8,128)(2,1)} %collective-permute-done.15.refs_3_), channel_id=1, source_target_pairs={{0,16},{16,0},{32,48},{48,32},{64,80},{80,64},{96,112},{112,96},{1... | collective-permute-start | bytes 3145736 | tf_op jit(solution)/shard_map/ppermute | solution.py:209
  68.3 1.0 copy-start.22
  72.9 21.0 %collective-permute-start.8 = (bf16[96,5248]{1,0:T(8,128)(2,1)}, bf16[96,5248]{1,0:T(8,128)(2,1)S(1)}, u32[]{:S(2)}, u32[]{:S(2)}) collective-permute-start(bf16[96,5248]{1,0:T(8,128)(2,1)} %collective-permute-done.6.refs_5_), channel_id=1, source_target_pairs={{0,4},{1,5},{2,6},{3,7},{4,8},{5,9},{6,10},{7,11},{8,12},{9,13},{1... | collective-permute-start | bytes 3022856 | tf_op jit(solution)/shard_map/ppermute | solution.py:212
  74.4 19.5 %collective-permute-start.10 = (bf16[96,5248]{1,0:T(8,128)(2,1)}, bf16[96,5248]{1,0:T(8,128)(2,1)S(1)}, u32[]{:S(2)}, u32[]{:S(2)}) collective-permute-start(bf16[96,5248]{1,0:T(8,128)(2,1)} %collective-permute-done.6.refs_5_), channel_id=1, source_target_pairs={{0,1},{1,2},{2,3},{3,0},{4,5},{5,6},{6,7},{7,4},{8,9},{9,10},{10,1... | collective-permute-start | bytes 3022856 | tf_op jit(solution)/shard_map/ppermute | solution.py:213
  75.7 32.9 %collective-permute-start.22 = (bf16[96,5248]{1,0:T(8,128)(2,1)}, bf16[96,5248]{1,0:T(8,128)(2,1)S(1)}, u32[]{:S(2)}, u32[]{:S(2)}) collective-permute-start(bf16[96,5248]{1,0:T(8,128)(2,1)} %collective-permute-done.17.refs_2_), channel_id=1, source_target_pairs={{0,1},{1,2},{2,3},{3,0},{4,5},{5,6},{6,7},{7,4},{8,9},{9,10},{10,1... | collective-permute-start | bytes 3022856 | tf_op jit(solution)/shard_map/ppermute | solution.py:213
  77.0 31.6 %collective-permute-start.21 = (bf16[96,5248]{1,0:T(8,128)(2,1)}, bf16[96,5248]{1,0:T(8,128)(2,1)S(1)}, u32[]{:S(2)}, u32[]{:S(2)}) collective-permute-start(bf16[96,5248]{1,0:T(8,128)(2,1)} %collective-permute-done.9.refs_3_), channel_id=1, source_target_pairs={{0,4},{1,5},{2,6},{3,7},{4,8},{5,9},{6,10},{7,11},{8,12},{9,13},{1... | collective-permute-start | bytes 3022856 | tf_op jit(solution)/shard_map/ppermute | solution.py:212
  78.3 1.2 %copy-start = (bf16[1024,512]{1,0:T(8,128)(2,1)S(1)}, bf16[1024,512]{1,0:T(8,128)(2,1)}, u32[]{:S(2)}) copy-start(bf16[1024,512]{1,0:T(8,128)(2,1)} %shard_map.47.refs_0_) | copy-start | bytes 3145732
  79.6 1.2 %copy-start.3 = (bf16[1024,512]{1,0:T(8,128)(2,1)S(1)}, bf16[1024,512]{1,0:T(8,128)(2,1)}, u32[]{:S(2)}) copy-start(bf16[1024,512]{1,0:T(8,128)(2,1)} %copy-done.2) | copy-start | bytes 3145732
  80.8 1.2 %copy-start.5 = (bf16[1024,512]{1,0:T(8,128)(2,1)S(1)}, bf16[1024,512]{1,0:T(8,128)(2,1)}, u32[]{:S(2)}) copy-start(bf16[1024,512]{1,0:T(8,128)(2,1)} %copy-done.4) | copy-start | bytes 3145732
  82.0 1.2 %copy-start.7 = (bf16[1024,512]{1,0:T(8,128)(2,1)S(1)}, bf16[1024,512]{1,0:T(8,128)(2,1)}, u32[]{:S(2)}) copy-start(bf16[1024,512]{1,0:T(8,128)(2,1)} %copy-done.6) | copy-start | bytes 3145732
  83.2 1.2 %copy-start.9 = (bf16[1024,512]{1,0:T(8,128)(2,1)S(1)}, bf16[1024,512]{1,0:T(8,128)(2,1)}, u32[]{:S(2)}) copy-start(bf16[1024,512]{1,0:T(8,128)(2,1)} %copy-done.8) | copy-start | bytes 3145732
  84.5 2.8 %copy-start.1 = (bf16[96,5248]{1,0:T(8,128)(2,1)S(1)}, bf16[96,5248]{1,0:T(8,128)(2,1)}, u32[]{:S(2)}) copy-start(bf16[96,5248]{1,0:T(8,128)(2,1)} %shard_map.46.refs_0_) | copy-start | bytes 3022852
  84.5 2.8 %copy-start.11 = (bf16[96,5248]{1,0:T(8,128)(2,1)S(1)}, bf16[96,5248]{1,0:T(8,128)(2,1)}, u32[]{:S(2)}) copy-start(bf16[96,5248]{1,0:T(8,128)(2,1)} %copy-done.10) | copy-start | bytes 3022852
  84.5 2.8 %copy-start.13 = (bf16[96,5248]{1,0:T(8,128)(2,1)S(1)}, bf16[96,5248]{1,0:T(8,128)(2,1)}, u32[]{:S(2)}) copy-start(bf16[96,5248]{1,0:T(8,128)(2,1)} %copy-done.12) | copy-start | bytes 3022852
  84.5 2.8 %copy-start.15 = (bf16[96,5248]{1,0:T(8,128)(2,1)S(1)}, bf16[96,5248]{1,0:T(8,128)(2,1)}, u32[]{:S(2)}) copy-start(bf16[96,5248]{1,0:T(8,128)(2,1)} %copy-done.14) | copy-start | bytes 3022852
  84.5 3.0 %copy-start.17 = (bf16[96,5248]{1,0:T(8,128)(2,1)S(1)}, bf16[96,5248]{1,0:T(8,128)(2,1)}, u32[]{:S(2)}) copy-start(bf16[96,5248]{1,0:T(8,128)(2,1)} %copy-done.16) | copy-start | bytes 3022852
  87.5 12.8 %copy-start.23 = (bf16[96,5248]{1,0:T(8,128)(2,1)S(1)}, bf16[96,5248]{1,0:T(8,128)(2,1)}, u32[]{:S(2)}) copy-start(bf16[96,5248]{1,0:T(8,128)(2,1)} %copy-done.22) | copy-start | bytes 3022852
  93.9 6.4 %copy-start.19 = (bf16[96,5248]{1,0:T(8,128)(2,1)S(1)}, bf16[96,5248]{1,0:T(8,128)(2,1)}, u32[]{:S(2)}) copy-start(bf16[96,5248]{1,0:T(8,128)(2,1)} %copy-done.18) | copy-start | bytes 3022852
  93.9 6.4 %copy-start.21 = (bf16[96,5248]{1,0:T(8,128)(2,1)S(1)}, bf16[96,5248]{1,0:T(8,128)(2,1)}, u32[]{:S(2)}) copy-start(bf16[96,5248]{1,0:T(8,128)(2,1)} %copy-done.20) | copy-start | bytes 3022852
  94.0 20.0 %collective-permute-start.19 = (bf16[48,5248]{1,0:T(8,128)(2,1)S(1)}, bf16[48,5248]{1,0:T(8,128)(2,1)S(1)}, u32[]{:S(2)}, u32[]{:S(2)}) collective-permute-start(bf16[48,5248]{1,0:T(8,128)(2,1)S(1)} %slice.10), channel_id=1, source_target_pairs={{0,1},{1,2},{2,3},{3,0},{4,5},{5,6},{6,7},{7,4},{8,9},{9,10},{10,1... | collective-permute-start | bytes 1511432 | tf_op jit(solution)/shard_map/ppermute | solution.py:213
  97.1 16.9 %collective-permute-start.20 = (bf16[48,5248]{1,0:T(8,128)(2,1)S(1)}, bf16[48,5248]{1,0:T(8,128)(2,1)S(1)}, u32[]{:S(2)}, u32[]{:S(2)}) collective-permute-start(bf16[48,5248]{1,0:T(8,128)(2,1)S(1)} %slice.11), channel_id=1, source_target_pairs={{0,4},{1,5},{2,6},{3,7},{4,8},{5,9},{6,10},{7,11},{8,12},{9,13},{1... | collective-permute-start | bytes 1511432 | tf_op jit(solution)/shard_map/ppermute | solution.py:212

commit v4 on v3

--- a/solution.py
+++ b/solution.py
@@ -63,18 +63,20 @@
             kept_ref[at] = ints_ref[at] * keep
 
 
-def mm_kernel(spots, chunks, offs, *refs):
+def mm_kernel(spots, offs, *refs):
     n = len(spots)
     amps, ints = refs[:n], refs[n]
     out, wide, done, out_sems = refs[-4:]
-    rows = amps[0].shape[0]
-    place = [pl.ds(i * rows, rows) for i in range(n)]
+    sizes = [v.shape[0] for v in amps]
+    begin = [sum(sizes[:i]) for i in range(n)]
+    place = [pl.ds(begin[i], sizes[i]) for i in range(n)]
     stores = [
-        pltpu.make_async_copy(done.at[place[i]], out.at[pl.ds(pl.multiple_of(offs[spots[i]], 16), rows)], out_sems.at[i])
+        pltpu.make_async_copy(done.at[place[i]], out.at[pl.ds(pl.multiple_of(offs[spots[i]], 16), sizes[i])], out_sems.at[i])
         for i in range(n)
     ]
     def fill(i):
-        here = slice(i * rows, (i + 1) * rows)
+        rows = sizes[i]
+        here = slice(begin[i], begin[i] + rows)
         code = amps[i][:, SLOTS * TILE :]
         zero = jnp.zeros((rows, TILE), BF)
         alpha = jnp.where(code < 0, zero, code)
@@ -94,20 +96,16 @@
                 v = jnp.where(beta <= t - FOLD, slot(t - FOLD), v)
             wide[here, t * TILE : (t + 1) * TILE] = v
 
-    first = 0
-    for size in chunks:
-        for i in range(first, first + size):
-            fill(i)
-        here = slice(first * rows, (first + size) * rows)
-        done[here, :] = jnp.dot(wide[here, :], ints[...], preferred_element_type=jnp.float32).astype(BF)
-        for i in range(first, first + size):
-            stores[i].start()
-        first += size
+    for i in range(n):
+        fill(i)
+    done[...] = jnp.dot(wide[...], ints[...], preferred_element_type=jnp.float32).astype(BF)
+    for store in stores:
+        store.start()
     for store in stores:
         store.wait()
 
 
-def multiply(amps, spots, chunks, offs, ints, out, out_rows):
+def multiply(amps, spots, offs, ints, out, out_rows):
     rows = sum(v.shape[0] for v in amps)
     cols = ints.shape[1]
     anywhere = pl.BlockSpec(memory_space=pl.ANY)
@@ -119,7 +117,7 @@
         alias = {len(args): 0}
         args.append(out)
     return pl.pallas_call(
-        functools.partial(mm_kernel, tuple(spots), tuple(chunks)),
+        functools.partial(mm_kernel, tuple(spots)),
         out_shape=jax.ShapeDtypeStruct((out_rows, cols), BF),
         in_specs=in_specs,
         out_specs=anywhere,
@@ -129,7 +127,7 @@
             pltpu.SemaphoreType.DMA((len(amps),)),
         ],
         input_output_aliases=alias,
-        compiler_params=pltpu.CompilerParams(vmem_limit_bytes=16 * 2**20),
+        compiler_params=pltpu.CompilerParams(vmem_limit_bytes=30 * 2**20),
         cost_estimate=pl.CostEstimate(
             flops=2 * rows * KT * TILE * cols,
             bytes_accessed=2 * (rows * WIDE + KT * TILE * cols + rows * cols),
@@ -232,13 +230,12 @@
 
     b13, b31 = by_x(after(b03, b12)), by_z(after(b30, b03))
     b32, b23 = by_x(after(b22, b12)), by_z(after(b22, b03))
-    out = multiply([own, b10, b01, b20, b02], [0, 4, 1, 8, 2], [5], offs, ints, None, total)
+    out = multiply([own, b10, b01, b20, b02], [0, 4, 1, 8, 2], offs, ints, None, total)
     half = dev_rows // 2
     b32, b23, out = lax.optimization_barrier((b32, b23, out))
     b33, b33_low = by_z(b32[:half]), by_x(b23[half:])
-    out = multiply([b11, b21, b30, b03, b12, b22], [5, 9, 12, 3, 6, 10], [6], offs, ints, out, total)
-    out = multiply([b13, b31, b32, b23], [7, 13, 14, 11], [4], offs, ints, out, total)
-    return multiply([b33, b33_low], [15, 16], [2], offs, ints, out, total)
+    out = multiply([b11, b21, b30, b03, b12, b22, b32, b23], [5, 9, 12, 3, 6, 10, 14, 11], offs, ints, out, total)
+    return multiply([b13, b31, b33, b33_low], [7, 13, 15, 16], offs, ints, out, total)
 
 
 def solution(mesh):

time: 117 us -> 117 us (level)
  local copies, waits for them, and re-layouts: 17.9 us -> 13.5 us
  waiting for transfers between devices: 43.6 us -> 47.8 us
    unnamed x48 -> x40, local copies, waits for them, and re-layouts: 17.2 us -> 10.7 us
    ppermute x8, waiting for transfers between devices: 22.3 us -> 24.7 us  [on_device(): by_z = lambda v: lax.ppermute(v, ('row', 'col'), along_z)]
    slice x2, local copies, waits for them, and re-layouts: 0.07 us -> 2.27 us  [on_device(): b33, b33_low = (by_z(b32[:half]), by_x(b23[half:]))]
    ppermute x8, waiting for transfers between devices: 15.9 us -> 18.1 us  [on_device(): by_x = lambda v: lax.ppermute(v, ('row', 'col'), along_x)]
    pallas_call x4 -> x3, Pallas kernels: 22.8 us -> 22.7 us  [multiply(): pl.pallas_call(functools.partial(mm_kernel, tuple(spots)), out_shape=jax....]
  transfers between devices with their start and end apart: 23 -> 23, of which waited for: 12 -> 12; matrix products, arithmetic and copies ran while one was open for 1% -> 3% of each run, Pallas kernels for 21% -> 20%
where the time goes in v4:
time: 117 us; the launch traced here: 116 us
  waiting for transfers between devices  47.8 us (41%)
  Pallas kernels  31 us (26%)
  starting transfers between devices  22.9 us (20%)
  local copies, waits for them, and re-layouts  13.5 us (12%)
    ppermute x8, waiting for transfers between devices, on_device(): by_z = lambda v: lax.ppermute(v, ('row', 'col'), along_z)  24.7 us
    pallas_call x3, Pallas kernels, multiply(): pl.pallas_call(functools.partial(mm_kernel, tuple(spots)), out_shape=jax....  22.7 us
    ppermute x8, waiting for transfers between devices, on_device(): by_x = lambda v: lax.ppermute(v, ('row', 'col'), along_x)  18.1 us
    ppermute x8, starting transfers between devices, on_device(): by_x = lambda v: lax.ppermute(v, ('row', 'col'), along_x)  13 us
    unnamed x40, local copies, waits for them, and re-layouts  10.7 us
    ppermute x8, starting transfers between devices, on_device(): by_z = lambda v: lax.ppermute(v, ('row', 'col'), along_z)  7.93 us
    ppermute x3, waiting for transfers between devices, on_device(): lax.ppermute(v, 'row', [(r, (r + (2 if r % 2 == 0 else -2)) % 8) for r in...  5.07 us
    pallas_call x1, Pallas kernels, pack(): pl.pallas_call(pack_kernel, out_shape=[jax.ShapeDtypeStruct((n, WIDE), BF...  3.41 us
  transfers between devices with their start and end apart: 23, of which 12 were waited for; matrix products, arithmetic and copies ran while one was open for 3% of the time, Pallas kernels for 20%

profile of v4, /device:TPU:34, one launch (start us, length us, event | category | flops | bytes accessed | tf_op | source)
XLA Modules:
  0.0 116.4 jit_solution(445274382911779241)
XLA Ops:
  0.0 3.4 %shard_map.46.refs_0_ = bf16[96,5248]{1,0:T(8,128)(2,1)} custom-call(s32[64,96]{1,0:T(8,128)} %bitcast.2, bf16[96,8192]{1,0:T(8,128)(2,1)} %amps_ref.1), custom_call_target="tpu_custom_call" | custom-call | tf_op jit(solution)/shard_map/pallas_call | solution.py:142
  3.4 1.9 %collective-permute-start = (bf16[96,5248]{1,0:T(8,128)(2,1)}, bf16[96,5248]{1,0:T(8,128)(2,1)}, u32[]{:S(2)}, u32[]{:S(2)}) collective-permute-start(bf16[96,5248]{1,0:T(8,128)(2,1)} %shard_map.46.refs_0_), channel_id=1, source_target_pairs={{0,1},{1,2},{2,3},{3,0},{4,5},{5,6},{6,7},{7,4},{8,9},{9,10},{10,1... | collective-permute-start | bytes 3022856 | tf_op jit(solution)/shard_map/ppermute | solution.py:211
  5.3 1.5 %collective-permute-start.1 = (bf16[96,5248]{1,0:T(8,128)(2,1)}, bf16[96,5248]{1,0:T(8,128)(2,1)}, u32[]{:S(2)}, u32[]{:S(2)}) collective-permute-start(bf16[96,5248]{1,0:T(8,128)(2,1)} %shard_map.46.refs_0_), channel_id=1, source_target_pairs={{0,4},{1,5},{2,6},{3,7},{4,8},{5,9},{6,10},{7,11},{8,12},{9,13},{1... | collective-permute-start | bytes 3022856 | tf_op jit(solution)/shard_map/ppermute | solution.py:210
  6.8 2.4 %shard_map.47.refs_0_ = bf16[1024,512]{1,0:T(8,128)(2,1)} custom-call(s32[4,8]{1,0:T(4,128)} %bitcast.3, bf16[1024,512]{1,0:T(8,128)(2,1)} %ints_ref.1), custom_call_target="tpu_custom_call" | custom-call | tf_op jit(solution)/shard_map/pallas_call | solution.py:149
  9.2 1.6 %collective-permute-start.14 = (bf16[1024,512]{1,0:T(8,128)(2,1)}, bf16[1024,512]{1,0:T(8,128)(2,1)S(1)}, u32[]{:S(2)}, u32[]{:S(2)}) collective-permute-start(bf16[1024,512]{1,0:T(8,128)(2,1)} %shard_map.47.refs_0_), channel_id=1, source_target_pairs={{0,32},{16,112},{32,64},{48,16},{64,96},{80,48},{96,0},{112,80},{1... | collective-permute-start | bytes 3145736 | tf_op jit(solution)/shard_map/ppermute | solution.py:206
  10.8 7.3 %collective-permute-done.refs_2_ = bf16[96,5248]{1,0:T(8,128)(2,1)} collective-permute-done((bf16[96,5248]{1,0:T(8,128)(2,1)}, bf16[96,5248]{1,0:T(8,128)(2,1)}, u32[]{:S(2)}, u32[]{:S(2)}) %collective-permute-start) | collective-permute-done | bytes 1007648 | tf_op jit(solution)/shard_map/ppermute | solution.py:211
  18.1 1.9 %collective-permute-done.1.refs_1_ = bf16[96,5248]{1,0:T(8,128)(2,1)} collective-permute-done((bf16[96,5248]{1,0:T(8,128)(2,1)}, bf16[96,5248]{1,0:T(8,128)(2,1)}, u32[]{:S(2)}, u32[]{:S(2)}) %collective-permute-start.1) | collective-permute-done | bytes 1007648 | tf_op jit(solution)/shard_map/ppermute | solution.py:210
  20.0 1.6 %collective-permute-start.2 = (bf16[96,5248]{1,0:T(8,128)(2,1)}, bf16[96,5248]{1,0:T(8,128)(2,1)S(1)}, u32[]{:S(2)}, u32[]{:S(2)}) collective-permute-start(bf16[96,5248]{1,0:T(8,128)(2,1)} %collective-permute-done.refs_2_), channel_id=1, source_target_pairs={{0,1},{1,2},{2,3},{3,0},{4,5},{5,6},{6,7},{7,4},{8,9},{9,10},{10,1... | collective-permute-start | bytes 3022856 | tf_op jit(solution)/shard_map/ppermute | solution.py:211
  21.6 1.5 %collective-permute-start.7 = (bf16[96,5248]{1,0:T(8,128)(2,1)}, bf16[96,5248]{1,0:T(8,128)(2,1)S(1)}, u32[]{:S(2)}, u32[]{:S(2)}) collective-permute-start(bf16[96,5248]{1,0:T(8,128)(2,1)} %collective-permute-done.1.refs_1_), channel_id=1, source_target_pairs={{0,4},{1,5},{2,6},{3,7},{4,8},{5,9},{6,10},{7,11},{8,12},{9,13},{1... | collective-permute-start | bytes 3022856 | tf_op jit(solution)/shard_map/ppermute | solution.py:210
  23.1 2.3 %collective-permute-done.14.refs_1_ = bf16[1024,512]{1,0:T(8,128)(2,1)S(1)} collective-permute-done((bf16[1024,512]{1,0:T(8,128)(2,1)}, bf16[1024,512]{1,0:T(8,128)(2,1)S(1)}, u32[]{:S(2)}, u32[]{:S(2)}) %collective-permute-start.14) | collective-permute-done | bytes 1048608 | tf_op jit(solution)/shard_map/ppermute | solution.py:206
  25.4 0.4 collective-permute-start.16
  25.8 1.2 %collective-permute-start.4 = (bf16[96,5248]{1,0:T(8,128)(2,1)}, bf16[96,5248]{1,0:T(8,128)(2,1)S(1)}, u32[]{:S(2)}, u32[]{:S(2)}) collective-permute-start(bf16[96,5248]{1,0:T(8,128)(2,1)} %collective-permute-done.refs_2_), channel_id=1, source_target_pairs={{0,4},{1,5},{2,6},{3,7},{4,8},{5,9},{6,10},{7,11},{8,12},{9,13},{1... | collective-permute-start | bytes 3022856 | tf_op jit(solution)/shard_map/ppermute | solution.py:210
  27.0 7.6 %collective-permute-done.2.refs_4_ = bf16[96,5248]{1,0:T(8,128)(2,1)S(1)} collective-permute-done((bf16[96,5248]{1,0:T(8,128)(2,1)}, bf16[96,5248]{1,0:T(8,128)(2,1)S(1)}, u32[]{:S(2)}, u32[]{:S(2)}) %collective-permute-start.2) | collective-permute-done | bytes 1007648 | tf_op jit(solution)/shard_map/ppermute | solution.py:211
  34.6 1.6 %collective-permute-done.7.refs_3_ = bf16[96,5248]{1,0:T(8,128)(2,1)S(1)} collective-permute-done((bf16[96,5248]{1,0:T(8,128)(2,1)}, bf16[96,5248]{1,0:T(8,128)(2,1)S(1)}, u32[]{:S(2)}, u32[]{:S(2)}) %collective-permute-start.7) | collective-permute-done | bytes 1007648 | tf_op jit(solution)/shard_map/ppermute | solution.py:210
  36.2 1.5 %collective-permute-start.8 = (bf16[96,5248]{1,0:T(8,128)(2,1)S(1)}, bf16[96,5248]{1,0:T(8,128)(2,1)S(1)}, u32[]{:S(2)}, u32[]{:S(2)}) collective-permute-start(bf16[96,5248]{1,0:T(8,128)(2,1)S(1)} %collective-permute-done.7.refs_3_), channel_id=1, source_target_pairs={{0,4},{1,5},{2,6},{3,7},{4,8},{5,9},{6,10},{7,11},{8,12},{9,13},{1... | collective-permute-start | bytes 3022856 | tf_op jit(solution)/shard_map/ppermute | solution.py:210
  37.7 1.0 copy-done.8
  38.7 2.8 %collective-permute-done.16.refs_2_ = bf16[1024,512]{1,0:T(8,128)(2,1)S(1)} collective-permute-done((bf16[1024,512]{1,0:T(8,128)(2,1)S(1)}, bf16[1024,512]{1,0:T(8,128)(2,1)S(1)}, u32[]{:S(2)}, u32[]{:S(2)}) %collective-permute-start.16) | collective-permute-done | bytes 1048608 | tf_op jit(solution)/shard_map/ppermute | solution.py:206
  41.4 1.0 copy-done.2
  42.4 4.6 %collective-permute-done.4.refs_0_ = bf16[96,5248]{1,0:T(8,128)(2,1)S(1)} collective-permute-done((bf16[96,5248]{1,0:T(8,128)(2,1)}, bf16[96,5248]{1,0:T(8,128)(2,1)S(1)}, u32[]{:S(2)}, u32[]{:S(2)}) %collective-permute-start.4) | collective-permute-done | bytes 1007648 | tf_op jit(solution)/shard_map/ppermute | solution.py:210
  47.0 1.0 copy-done.10
  48.0 2.5 %collective-permute-done.10.refs_1_ = bf16[96,5248]{1,0:T(8,128)(2,1)S(1)} collective-permute-done((bf16[96,5248]{1,0:T(8,128)(2,1)S(1)}, bf16[96,5248]{1,0:T(8,128)(2,1)S(1)}, u32[]{:S(2)}, u32[]{:S(2)}) %collective-permute-start.10) | collective-permute-done | bytes 1007648 | tf_op jit(solution)/shard_map/ppermute | solution.py:211
  50.6 1.5 %collective-permute-start.5 = (bf16[96,5248]{1,0:T(8,128)(2,1)S(1)}, bf16[96,5248]{1,0:T(8,128)(2,1)S(1)}, u32[]{:S(2)}, u32[]{:S(2)}) collective-permute-start(bf16[96,5248]{1,0:T(8,128)(2,1)S(1)} %collective-permute-done.2.refs_4_), channel_id=1, source_target_pairs={{0,4},{1,5},{2,6},{3,7},{4,8},{5,9},{6,10},{7,11},{8,12},{9,13},{1... | collective-permute-start | bytes 3022856 | tf_op jit(solution)/shard_map/ppermute | solution.py:210
  52.1 1.0 copy-done.6
  53.0 4.8 %collective-permute-done.8.refs_2_ = bf16[96,5248]{1,0:T(8,128)(2,1)S(1)} collective-permute-done((bf16[96,5248]{1,0:T(8,128)(2,1)S(1)}, bf16[96,5248]{1,0:T(8,128)(2,1)S(1)}, u32[]{:S(2)}, u32[]{:S(2)}) %collective-permute-start.8) | collective-permute-done | bytes 1007648 | tf_op jit(solution)/shard_map/ppermute | solution.py:210
  57.8 0.0 collective-permute-start.11
  57.8 1.1 copy-done.14
  58.9 3.5 %collective-permute-done.3.refs_3_ = bf16[96,5248]{1,0:T(8,128)(2,1)S(1)} collective-permute-done((bf16[96,5248]{1,0:T(8,128)(2,1)S(1)}, bf16[96,5248]{1,0:T(8,128)(2,1)S(1)}, u32[]{:S(2)}, u32[]{:S(2)}) %collective-permute-start.3) | collective-permute-done | bytes 1007648 | tf_op jit(solution)/shard_map/ppermute | solution.py:211
  62.4 1.0 copy-done.4
  63.4 5.2 %collective-permute-done.5.refs_4_ = bf16[96,5248]{1,0:T(8,128)(2,1)S(1)} collective-permute-done((bf16[96,5248]{1,0:T(8,128)(2,1)S(1)}, bf16[96,5248]{1,0:T(8,128)(2,1)S(1)}, u32[]{:S(2)}, u32[]{:S(2)}) %collective-permute-start.5) | collective-permute-done | bytes 1007648 | tf_op jit(solution)/shard_map/ppermute | solution.py:210
  68.6 1.0 copy-done.18
  69.6 3.7 %collective-permute-done.11.refs_5_ = bf16[96,5248]{1,0:T(8,128)(2,1)} collective-permute-done((bf16[96,5248]{1,0:T(8,128)(2,1)S(1)}, bf16[96,5248]{1,0:T(8,128)(2,1)}, u32[]{:S(2)}, u32[]{:S(2)}) %collective-permute-start.11) | collective-permute-done | bytes 1007648 | tf_op jit(solution)/shard_map/ppermute | solution.py:211
  73.3 1.5 %collective-permute-start.12 = (bf16[96,5248]{1,0:T(8,128)(2,1)}, bf16[96,5248]{1,0:T(8,128)(2,1)}, u32[]{:S(2)}, u32[]{:S(2)}) collective-permute-start(bf16[96,5248]{1,0:T(8,128)(2,1)} %collective-permute-done.11.refs_5_), channel_id=1, source_target_pairs={{0,4},{1,5},{2,6},{3,7},{4,8},{5,9},{6,10},{7,11},{8,12},{9,13},{1... | collective-permute-start | bytes 3022856 | tf_op jit(solution)/shard_map/ppermute | solution.py:210
  74.8 0.6 slice.9
  75.9 0.1 pad_add_fusion.offs
  76.0 1.3 %collective-permute-start.9 = (bf16[96,5248]{1,0:T(8,128)(2,1)}, bf16[96,5248]{1,0:T(8,128)(2,1)S(1)}, u32[]{:S(2)}, u32[]{:S(2)}) collective-permute-start(bf16[96,5248]{1,0:T(8,128)(2,1)} %copy-done.12), channel_id=1, source_target_pairs={{0,1},{1,2},{2,3},{3,0},{4,5},{5,6},{6,7},{7,4},{8,9},{9,10},{10,1... | collective-permute-start | bytes 3022856 | tf_op jit(solution)/shard_map/ppermute | solution.py:211
  77.3 1.2 %collective-permute-start.6 = (bf16[96,5248]{1,0:T(8,128)(2,1)}, bf16[96,5248]{1,0:T(8,128)(2,1)S(1)}, u32[]{:S(2)}, u32[]{:S(2)}) collective-permute-start(bf16[96,5248]{1,0:T(8,128)(2,1)} %copy-done.16), channel_id=1, source_target_pairs={{0,4},{1,5},{2,6},{3,7},{4,8},{5,9},{6,10},{7,11},{8,12},{9,13},{1... | collective-permute-start | bytes 3022856 | tf_op jit(solution)/shard_map/ppermute | solution.py:210
  78.5 0.1 pad_add_fusion.1.offs
  78.5 1.2 %copy-done = bf16[1024,512]{1,0:T(8,128)(2,1)S(1)} copy-done((bf16[1024,512]{1,0:T(8,128)(2,1)S(1)}, bf16[1024,512]{1,0:T(8,128)(2,1)}, u32[]{:S(2)}) %copy-start) | copy-done | bytes 1048600
  79.8 1.2 %copy-done.3 = bf16[1024,512]{1,0:T(8,128)(2,1)S(1)} copy-done((bf16[1024,512]{1,0:T(8,128)(2,1)S(1)}, bf16[1024,512]{1,0:T(8,128)(2,1)}, u32[]{:S(2)}) %copy-start.3) | copy-done | bytes 1048600
  81.0 1.2 %copy-done.5 = bf16[1024,512]{1,0:T(8,128)(2,1)S(1)} copy-done((bf16[1024,512]{1,0:T(8,128)(2,1)S(1)}, bf16[1024,512]{1,0:T(8,128)(2,1)}, u32[]{:S(2)}) %copy-start.5) | copy-done | bytes 1048600
  82.2 2.5 %shard_map.48.refs_5_.refs_8_.refs_4_ = bf16[8192,512]{1,0:T(8,128)(2,1)S(1)} custom-call(s32[8]{0:T(128)S(1)} %pad_add_fusion.1.offs, bf16[1024,512]{1,0:T(8,128)(2,1)S(1)} %copy-done, bf16[1024,512]{1,0:T(8,128)(2,1)S(1)} %collective-permute-done.14.refs_1_, bf16[1024,512]{1,0:T(8,128)(2,1)S(1)} %collective-permute-done.16.refs_2_, ...), custom_call_target="tpu_custom_call" | custom-call | tf_op jit(solution)/shard_map/pallas_call | solution.py:185
  84.8 7.6 %shard_map.49.refs_9_ = bf16[1536,512]{1,0:T(8,128)(2,1)} custom-call(s32[17]{0:T(128)S(1)} %pad_add_fusion.offs, bf16[96,5248]{1,0:T(8,128)(2,1)S(1)} %copy-done.1, bf16[96,5248]{1,0:T(8,128)(2,1)} %collective-permute-done.1.refs_1_, bf16[96,5248]{1,0:T(8,128)(2,1)} %collective-permute-done.refs_2_, bf16[96,5248]{1,0:T(8,128)(2,1)S(1)} %copy-done.9, ...), custom_call_target="tpu_custom_call" | custom-call | flops 4026531840 | bytes 13918208 | tf_op jit(solution)/shard_map/pallas_call | solution.py:119
  92.4 1.2 %slice.10 = bf16[48,5248]{1,0:T(8,128)(2,1)S(1)} slice(bf16[96,5248]{1,0:T(8,128)(2,1)} %collective-permute-done.12.refs_6_), slice={[0:48], [0:5248]} | slice | bytes 1007616 | tf_op jit(solution)/shard_map/slice | solution.py:236
  93.6 3.1 %collective-permute-start.21 = (bf16[48,5248]{1,0:T(8,128)(2,1)S(1)}, bf16[48,5248]{1,0:T(8,128)(2,1)S(1)}, u32[]{:S(2)}, u32[]{:S(2)}) collective-permute-start(bf16[48,5248]{1,0:T(8,128)(2,1)S(1)} %slice.10), channel_id=1, source_target_pairs={{0,1},{1,2},{2,3},{3,0},{4,5},{5,6},{6,7},{7,4},{8,9},{9,10},{10,1... | collective-permute-start | bytes 1511432 | tf_op jit(solution)/shard_map/ppermute | solution.py:211
  96.7 1.1 slice.11
  97.8 3.2 %collective-permute-start.22 = (bf16[48,5248]{1,0:T(8,128)(2,1)S(1)}, bf16[48,5248]{1,0:T(8,128)(2,1)S(1)}, u32[]{:S(2)}, u32[]{:S(2)}) collective-permute-start(bf16[48,5248]{1,0:T(8,128)(2,1)S(1)} %slice.11), channel_id=1, source_target_pairs={{0,4},{1,5},{2,6},{3,7},{4,8},{5,9},{6,10},{7,11},{8,12},{9,13},{1... | collective-permute-start | bytes 1511432 | tf_op jit(solution)/shard_map/ppermute | solution.py:210
  101.0 10.5 %shard_map.50.refs_5_ = bf16[1536,512]{1,0:T(8,128)(2,1)} custom-call(s32[17]{0:T(128)S(1)} %pad_add_fusion.offs, bf16[96,5248]{1,0:T(8,128)(2,1)S(1)} %copy-done.11, bf16[96,5248]{1,0:T(8,128)(2,1)S(1)} %copy-done.15, bf16[96,5248]{1,0:T(8,128)(2,1)S(1)} %copy-done.13, bf16[96,5248]{1,0:T(8,128)(2,1)S(1)} %copy-done.17, ...), custom_call_target="tpu_custom_call", output_to_operand_aliasing={{}: (10, {})} | custom-call | flops 6442450944 | bytes 17235968 | tf_op jit(solution)/shard_map/pallas_call | solution.py:119
  111.6 4.6 %shard_map.51 = bf16[1536,512]{1,0:T(8,128)(2,1)} custom-call(s32[17]{0:T(128)S(1)} %pad_add_fusion.offs, bf16[96,5248]{1,0:T(8,128)(2,1)S(1)} %collective-permute-done.6.refs_0_, bf16[96,5248]{1,0:T(8,128)(2,1)S(1)} %collective-permute-done.9.refs_1_, bf16[48,5248]{1,0:T(8,128)(2,1)S(1)} %collective-permute-done.21.refs_2_, ...), custom_call_target="tpu_custom_call", output_to_operand_aliasing={{}: (6, {})} | custom-call | flops 2415919104 | bytes 11706368 | tf_op jit(solution)/shard_map/pallas_call | solution.py:119
  (51 shorter events, 0.1 us)
Async XLA Ops:
  3.4 14.7 %collective-permute-start = (bf16[96,5248]{1,0:T(8,128)(2,1)}, bf16[96,5248]{1,0:T(8,128)(2,1)}, u32[]{:S(2)}, u32[]{:S(2)}) collective-permute-start(bf16[96,5248]{1,0:T(8,128)(2,1)} %shard_map.46.refs_0_), channel_id=1, source_target_pairs={{0,1},{1,2},{2,3},{3,0},{4,5},{5,6},{6,7},{7,4},{8,9},{9,10},{10,1... | collective-permute-start | bytes 3022856 | tf_op jit(solution)/shard_map/ppermute | solution.py:211
  5.3 14.7 %collective-permute-start.1 = (bf16[96,5248]{1,0:T(8,128)(2,1)}, bf16[96,5248]{1,0:T(8,128)(2,1)}, u32[]{:S(2)}, u32[]{:S(2)}) collective-permute-start(bf16[96,5248]{1,0:T(8,128)(2,1)} %shard_map.46.refs_0_), channel_id=1, source_target_pairs={{0,4},{1,5},{2,6},{3,7},{4,8},{5,9},{6,10},{7,11},{8,12},{9,13},{1... | collective-permute-start | bytes 3022856 | tf_op jit(solution)/shard_map/ppermute | solution.py:210
  9.2 16.2 %collective-permute-start.14 = (bf16[1024,512]{1,0:T(8,128)(2,1)}, bf16[1024,512]{1,0:T(8,128)(2,1)S(1)}, u32[]{:S(2)}, u32[]{:S(2)}) collective-permute-start(bf16[1024,512]{1,0:T(8,128)(2,1)} %shard_map.47.refs_0_), channel_id=1, source_target_pairs={{0,32},{16,112},{32,64},{48,16},{64,96},{80,48},{96,0},{112,80},{1... | collective-permute-start | bytes 3145736 | tf_op jit(solution)/shard_map/ppermute | solution.py:206
  10.8 14.6 %collective-permute-start.15 = (bf16[1024,512]{1,0:T(8,128)(2,1)}, bf16[1024,512]{1,0:T(8,128)(2,1)S(1)}, u32[]{:S(2)}, u32[]{:S(2)}) collective-permute-start(bf16[1024,512]{1,0:T(8,128)(2,1)} %shard_map.47.refs_0_), channel_id=1, source_target_pairs={{0,16},{16,0},{32,48},{48,32},{64,80},{80,64},{96,112},{112,96},{1... | collective-permute-start | bytes 3145736 | tf_op jit(solution)/shard_map/ppermute | solution.py:207
  20.0 14.6 %collective-permute-start.2 = (bf16[96,5248]{1,0:T(8,128)(2,1)}, bf16[96,5248]{1,0:T(8,128)(2,1)S(1)}, u32[]{:S(2)}, u32[]{:S(2)}) collective-permute-start(bf16[96,5248]{1,0:T(8,128)(2,1)} %collective-permute-done.refs_2_), channel_id=1, source_target_pairs={{0,1},{1,2},{2,3},{3,0},{4,5},{5,6},{6,7},{7,4},{8,9},{9,10},{10,1... | collective-permute-start | bytes 3022856 | tf_op jit(solution)/shard_map/ppermute | solution.py:211
  21.6 14.6 %collective-permute-start.7 = (bf16[96,5248]{1,0:T(8,128)(2,1)}, bf16[96,5248]{1,0:T(8,128)(2,1)S(1)}, u32[]{:S(2)}, u32[]{:S(2)}) collective-permute-start(bf16[96,5248]{1,0:T(8,128)(2,1)} %collective-permute-done.1.refs_1_), channel_id=1, source_target_pairs={{0,4},{1,5},{2,6},{3,7},{4,8},{5,9},{6,10},{7,11},{8,12},{9,13},{1... | collective-permute-start | bytes 3022856 | tf_op jit(solution)/shard_map/ppermute | solution.py:210
  25.4 16.0 %collective-permute-start.16 = (bf16[1024,512]{1,0:T(8,128)(2,1)S(1)}, bf16[1024,512]{1,0:T(8,128)(2,1)S(1)}, u32[]{:S(2)}, u32[]{:S(2)}) collective-permute-start(bf16[1024,512]{1,0:T(8,128)(2,1)S(1)} %collective-permute-done.14.refs_1_), channel_id=1, source_target_pairs={{0,32},{16,112},{32,64},{48,16},{64,96},{80,48},{96,0},{112,80},{1... | collective-permute-start | bytes 3145736 | tf_op jit(solution)/shard_map/ppermute | solution.py:206
  25.8 15.6 %collective-permute-start.17 = (bf16[1024,512]{1,0:T(8,128)(2,1)S(1)}, bf16[1024,512]{1,0:T(8,128)(2,1)S(1)}, u32[]{:S(2)}, u32[]{:S(2)}) collective-permute-start(bf16[1024,512]{1,0:T(8,128)(2,1)S(1)} %collective-permute-done.14.refs_1_), channel_id=1, source_target_pairs={{0,16},{16,0},{32,48},{48,32},{64,80},{80,64},{96,112},{112,96},{1... | collective-permute-start | bytes 3145736 | tf_op jit(solution)/shard_map/ppermute | solution.py:207
  25.8 21.2 %collective-permute-start.4 = (bf16[96,5248]{1,0:T(8,128)(2,1)}, bf16[96,5248]{1,0:T(8,128)(2,1)S(1)}, u32[]{:S(2)}, u32[]{:S(2)}) collective-permute-start(bf16[96,5248]{1,0:T(8,128)(2,1)} %collective-permute-done.refs_2_), channel_id=1, source_target_pairs={{0,4},{1,5},{2,6},{3,7},{4,8},{5,9},{6,10},{7,11},{8,12},{9,13},{1... | collective-permute-start | bytes 3022856 | tf_op jit(solution)/shard_map/ppermute | solution.py:210
  36.2 14.4 %collective-permute-start.10 = (bf16[96,5248]{1,0:T(8,128)(2,1)S(1)}, bf16[96,5248]{1,0:T(8,128)(2,1)S(1)}, u32[]{:S(2)}, u32[]{:S(2)}) collective-permute-start(bf16[96,5248]{1,0:T(8,128)(2,1)S(1)} %collective-permute-done.7.refs_3_), channel_id=1, source_target_pairs={{0,1},{1,2},{2,3},{3,0},{4,5},{5,6},{6,7},{7,4},{8,9},{9,10},{10,1... | collective-permute-start | bytes 3022856 | tf_op jit(solution)/shard_map/ppermute | solution.py:211
  36.2 21.6 %collective-permute-start.8 = (bf16[96,5248]{1,0:T(8,128)(2,1)S(1)}, bf16[96,5248]{1,0:T(8,128)(2,1)S(1)}, u32[]{:S(2)}, u32[]{:S(2)}) collective-permute-start(bf16[96,5248]{1,0:T(8,128)(2,1)S(1)} %collective-permute-done.7.refs_3_), channel_id=1, source_target_pairs={{0,4},{1,5},{2,6},{3,7},{4,8},{5,9},{6,10},{7,11},{8,12},{9,13},{1... | collective-permute-start | bytes 3022856 | tf_op jit(solution)/shard_map/ppermute | solution.py:210
  37.7 1.0 copy-start.8
  41.4 1.0 copy-start.2
  42.4 20.0 %collective-permute-start.18 = (bf16[1024,512]{1,0:T(8,128)(2,1)S(1)}, bf16[1024,512]{1,0:T(8,128)(2,1)}, u32[]{:S(2)}, u32[]{:S(2)}) collective-permute-start(bf16[1024,512]{1,0:T(8,128)(2,1)S(1)} %collective-permute-done.16.refs_2_), channel_id=1, source_target_pairs={{0,32},{16,112},{32,64},{48,16},{64,96},{80,48},{96,0},{112,80},{1... | collective-permute-start | bytes 3145736 | tf_op jit(solution)/shard_map/ppermute | solution.py:206
  42.4 20.0 %collective-permute-start.19 = (bf16[1024,512]{1,0:T(8,128)(2,1)S(1)}, bf16[1024,512]{1,0:T(8,128)(2,1)S(1)}, u32[]{:S(2)}, u32[]{:S(2)}) collective-permute-start(bf16[1024,512]{1,0:T(8,128)(2,1)S(1)} %collective-permute-done.16.refs_2_), channel_id=1, source_target_pairs={{0,16},{16,0},{32,48},{48,32},{64,80},{80,64},{96,112},{112,96},{1... | collective-permute-start | bytes 3145736 | tf_op jit(solution)/shard_map/ppermute | solution.py:207
  47.0 1.0 copy-start.10
  48.0 14.4 %collective-permute-start.3 = (bf16[96,5248]{1,0:T(8,128)(2,1)S(1)}, bf16[96,5248]{1,0:T(8,128)(2,1)S(1)}, u32[]{:S(2)}, u32[]{:S(2)}) collective-permute-start(bf16[96,5248]{1,0:T(8,128)(2,1)S(1)} %collective-permute-done.2.refs_4_), channel_id=1, source_target_pairs={{0,1},{1,2},{2,3},{3,0},{4,5},{5,6},{6,7},{7,4},{8,9},{9,10},{10,1... | collective-permute-start | bytes 3022856 | tf_op jit(solution)/shard_map/ppermute | solution.py:211
  50.6 18.0 %collective-permute-start.5 = (bf16[96,5248]{1,0:T(8,128)(2,1)S(1)}, bf16[96,5248]{1,0:T(8,128)(2,1)S(1)}, u32[]{:S(2)}, u32[]{:S(2)}) collective-permute-start(bf16[96,5248]{1,0:T(8,128)(2,1)S(1)} %collective-permute-done.2.refs_4_), channel_id=1, source_target_pairs={{0,4},{1,5},{2,6},{3,7},{4,8},{5,9},{6,10},{7,11},{8,12},{9,13},{1... | collective-permute-start | bytes 3022856 | tf_op jit(solution)/shard_map/ppermute | solution.py:210
  52.1 1.0 copy-start.6
  57.8 10.8 %copy-start.12 = (bf16[96,5248]{1,0:T(8,128)(2,1)}, bf16[96,5248]{1,0:T(8,128)(2,1)S(1)}, u32[]{:S(2)}) copy-start(bf16[96,5248]{1,0:T(8,128)(2,1)S(1)} %collective-permute-done.8.refs_2_) | copy-start | bytes 3022852
  57.8 15.5 %collective-permute-start.11 = (bf16[96,5248]{1,0:T(8,128)(2,1)S(1)}, bf16[96,5248]{1,0:T(8,128)(2,1)}, u32[]{:S(2)}, u32[]{:S(2)}) collective-permute-start(bf16[96,5248]{1,0:T(8,128)(2,1)S(1)} %collective-permute-done.10.refs_1_), channel_id=1, source_target_pairs={{0,1},{1,2},{2,3},{3,0},{4,5},{5,6},{6,7},{7,4},{8,9},{9,10},{10,1... | collective-permute-start | bytes 3022856 | tf_op jit(solution)/shard_map/ppermute | solution.py:211
  57.8 1.1 copy-start.14
  62.4 10.9 %copy-start.16 = (bf16[96,5248]{1,0:T(8,128)(2,1)}, bf16[96,5248]{1,0:T(8,128)(2,1)S(1)}, u32[]{:S(2)}) copy-start(bf16[96,5248]{1,0:T(8,128)(2,1)S(1)} %collective-permute-done.3.refs_3_) | copy-start | bytes 3022852
  62.4 1.0 copy-start.4
  63.4 15.1 %collective-permute-start.20 = (bf16[1024,512]{1,0:T(8,128)(2,1)}, bf16[1024,512]{1,0:T(8,128)(2,1)}, u32[]{:S(2)}, u32[]{:S(2)}) collective-permute-start(bf16[1024,512]{1,0:T(8,128)(2,1)} %collective-permute-done.18.refs_3_), channel_id=1, source_target_pairs={{0,16},{16,0},{32,48},{48,32},{64,80},{80,64},{96,112},{112,96},{1... | collective-permute-start | bytes 3145736 | tf_op jit(solution)/shard_map/ppermute | solution.py:207
  68.6 1.0 copy-start.18
  73.3 19.1 %collective-permute-start.12 = (bf16[96,5248]{1,0:T(8,128)(2,1)}, bf16[96,5248]{1,0:T(8,128)(2,1)}, u32[]{:S(2)}, u32[]{:S(2)}) collective-permute-start(bf16[96,5248]{1,0:T(8,128)(2,1)} %collective-permute-done.11.refs_5_), channel_id=1, source_target_pairs={{0,4},{1,5},{2,6},{3,7},{4,8},{5,9},{6,10},{7,11},{8,12},{9,13},{1... | collective-permute-start | bytes 3022856 | tf_op jit(solution)/shard_map/ppermute | solution.py:210
  74.8 17.7 %collective-permute-start.13 = (bf16[96,5248]{1,0:T(8,128)(2,1)}, bf16[96,5248]{1,0:T(8,128)(2,1)}, u32[]{:S(2)}, u32[]{:S(2)}) collective-permute-start(bf16[96,5248]{1,0:T(8,128)(2,1)} %collective-permute-done.11.refs_5_), channel_id=1, source_target_pairs={{0,1},{1,2},{2,3},{3,0},{4,5},{5,6},{6,7},{7,4},{8,9},{9,10},{10,1... | collective-permute-start | bytes 3022856 | tf_op jit(solution)/shard_map/ppermute | solution.py:211
  76.0 35.6 %collective-permute-start.9 = (bf16[96,5248]{1,0:T(8,128)(2,1)}, bf16[96,5248]{1,0:T(8,128)(2,1)S(1)}, u32[]{:S(2)}, u32[]{:S(2)}) collective-permute-start(bf16[96,5248]{1,0:T(8,128)(2,1)} %copy-done.12), channel_id=1, source_target_pairs={{0,1},{1,2},{2,3},{3,0},{4,5},{5,6},{6,7},{7,4},{8,9},{9,10},{10,1... | collective-permute-start | bytes 3022856 | tf_op jit(solution)/shard_map/ppermute | solution.py:211
  77.3 34.3 %collective-permute-start.6 = (bf16[96,5248]{1,0:T(8,128)(2,1)}, bf16[96,5248]{1,0:T(8,128)(2,1)S(1)}, u32[]{:S(2)}, u32[]{:S(2)}) collective-permute-start(bf16[96,5248]{1,0:T(8,128)(2,1)} %copy-done.16), channel_id=1, source_target_pairs={{0,4},{1,5},{2,6},{3,7},{4,8},{5,9},{6,10},{7,11},{8,12},{9,13},{1... | collective-permute-start | bytes 3022856 | tf_op jit(solution)/shard_map/ppermute | solution.py:210
  78.5 1.2 %copy-start = (bf16[1024,512]{1,0:T(8,128)(2,1)S(1)}, bf16[1024,512]{1,0:T(8,128)(2,1)}, u32[]{:S(2)}) copy-start(bf16[1024,512]{1,0:T(8,128)(2,1)} %shard_map.47.refs_0_) | copy-start | bytes 3145732
  79.8 1.2 %copy-start.3 = (bf16[1024,512]{1,0:T(8,128)(2,1)S(1)}, bf16[1024,512]{1,0:T(8,128)(2,1)}, u32[]{:S(2)}) copy-start(bf16[1024,512]{1,0:T(8,128)(2,1)} %copy-done.2) | copy-start | bytes 3145732
  81.0 1.2 %copy-start.5 = (bf16[1024,512]{1,0:T(8,128)(2,1)S(1)}, bf16[1024,512]{1,0:T(8,128)(2,1)}, u32[]{:S(2)}) copy-start(bf16[1024,512]{1,0:T(8,128)(2,1)} %copy-done.4) | copy-start | bytes 3145732
  82.2 2.5 %copy-start.1 = (bf16[96,5248]{1,0:T(8,128)(2,1)S(1)}, bf16[96,5248]{1,0:T(8,128)(2,1)}, u32[]{:S(2)}) copy-start(bf16[96,5248]{1,0:T(8,128)(2,1)} %shard_map.46.refs_0_) | copy-start | bytes 3022852
  82.2 2.6 %copy-start.7 = (bf16[96,5248]{1,0:T(8,128)(2,1)S(1)}, bf16[96,5248]{1,0:T(8,128)(2,1)}, u32[]{:S(2)}) copy-start(bf16[96,5248]{1,0:T(8,128)(2,1)} %copy-done.6) | copy-start | bytes 3022852
  82.2 2.6 %copy-start.9 = (bf16[96,5248]{1,0:T(8,128)(2,1)S(1)}, bf16[96,5248]{1,0:T(8,128)(2,1)}, u32[]{:S(2)}) copy-start(bf16[96,5248]{1,0:T(8,128)(2,1)} %copy-done.8) | copy-start | bytes 3022852
  84.8 16.2 %copy-start.15 = (bf16[96,5248]{1,0:T(8,128)(2,1)S(1)}, bf16[96,5248]{1,0:T(8,128)(2,1)}, u32[]{:S(2)}) copy-start(bf16[96,5248]{1,0:T(8,128)(2,1)} %copy-done.14) | copy-start | bytes 3022852
  84.8 16.2 %copy-start.17 = (bf16[96,5248]{1,0:T(8,128)(2,1)S(1)}, bf16[96,5248]{1,0:T(8,128)(2,1)}, u32[]{:S(2)}) copy-start(bf16[96,5248]{1,0:T(8,128)(2,1)} %copy-done.16) | copy-start | bytes 3022852
  84.8 16.2 %copy-start.19 = (bf16[96,5248]{1,0:T(8,128)(2,1)S(1)}, bf16[96,5248]{1,0:T(8,128)(2,1)}, u32[]{:S(2)}) copy-start(bf16[96,5248]{1,0:T(8,128)(2,1)} %copy-done.18) | copy-start | bytes 3022852
  92.4 8.6 %copy-start.11 = (bf16[96,5248]{1,0:T(8,128)(2,1)S(1)}, bf16[96,5248]{1,0:T(8,128)(2,1)}, u32[]{:S(2)}) copy-start(bf16[96,5248]{1,0:T(8,128)(2,1)} %copy-done.10) | copy-start | bytes 3022852
  92.4 8.6 %copy-start.13 = (bf16[96,5248]{1,0:T(8,128)(2,1)S(1)}, bf16[96,5248]{1,0:T(8,128)(2,1)}, u32[]{:S(2)}) copy-start(bf16[96,5248]{1,0:T(8,128)(2,1)} %copy-done.12) | copy-start | bytes 3022852
  93.6 17.9 %collective-permute-start.21 = (bf16[48,5248]{1,0:T(8,128)(2,1)S(1)}, bf16[48,5248]{1,0:T(8,128)(2,1)S(1)}, u32[]{:S(2)}, u32[]{:S(2)}) collective-permute-start(bf16[48,5248]{1,0:T(8,128)(2,1)S(1)} %slice.10), channel_id=1, source_target_pairs={{0,1},{1,2},{2,3},{3,0},{4,5},{5,6},{6,7},{7,4},{8,9},{9,10},{10,1... | collective-permute-start | bytes 1511432 | tf_op jit(solution)/shard_map/ppermute | solution.py:211
  97.8 13.8 %collective-permute-start.22 = (bf16[48,5248]{1,0:T(8,128)(2,1)S(1)}, bf16[48,5248]{1,0:T(8,128)(2,1)S(1)}, u32[]{:S(2)}, u32[]{:S(2)}) collective-permute-start(bf16[48,5248]{1,0:T(8,128)(2,1)S(1)} %slice.11), channel_id=1, source_target_pairs={{0,4},{1,5},{2,6},{3,7},{4,8},{5,9},{6,10},{7,11},{8,12},{9,13},{1... | collective-permute-start | bytes 1511432 | tf_op jit(solution)/shard_map/ppermute | solution.py:210
